TPU v7x, 512 devices: a whole 4x4x16 slice. The times are simulated.
512 devices in a mesh: blk: 64 (over z, y_lo, core), member: 8 (over x, y_hi).
Axes of the slice: x: 4, y: 4 (y_hi: 2, y_lo: 2; y = y_hi * 2 + y_lo), z: 16, core: 2. Of those that a mesh axis runs over, the one named last changes fastest.
Arguments:
- images: bfloat16 [65536, 1152], P(('blk', 'member')), may hold values from -2.5 to 2.5
- texts: bfloat16 [65536, 1152], P(('blk', 'member')), may hold values from -2.5 to 2.5
- log_scale: float32 [1], replicated, may hold values from 2 to 2.6
- bias: float32 [1], replicated, may hold values from -6 to -4
Outputs:
- image_grad: float32 [65536, 1152], P(('blk', 'member'))
- text_grad: float32 [65536, 1152], P(('blk', 'member'))
- text_loss: float32 [65536], P(('blk', 'member'))
All inputs are finite; a program needn't handle non-finite values.
Results may differ from a plain program's by a relative error of at most 0.02.
Values may be sent and summed in bfloat16 or wider, within the bound.
A program may use at most 64 MiB of HBM per device.

v0:
```python
import jax
import jax.numpy as jnp
from jax import lax
from jax.sharding import PartitionSpec as P

STEPS = 8


def shifted(block, axis, distance):
    devices = range(lax.axis_size(axis))
    route = [((i - distance) % len(devices), i) for i in devices]
    return lax.ppermute(block, axis, route)


def normalize(values):
    wide = values.astype(jnp.float32)
    inverse = lax.rsqrt(jnp.sum(wide * wide, axis=-1, keepdims=True) + 1e-06)
    return (wide * inverse, inverse)


def chain_back(unit, inverse, upstream):
    return inverse * (upstream - unit * jnp.sum(unit * upstream, axis=-1, keepdims=True))


def text_term(slope, group):
    return lax.dot_general(
        slope, group, (((0,), (0,)), ((), ())), preferred_element_type=jnp.float32
    )


def on_device(images, texts, log_scale, bias):
    pairs = images.shape[0]
    width = images.shape[1]
    temper = jnp.exp(log_scale[0])
    offset = bias[0]
    image_unit, image_inv = normalize(images)
    text_unit, text_inv = normalize(texts)
    image_low = image_unit.astype(jnp.bfloat16)
    current = text_unit.astype(jnp.bfloat16)
    group = lax.all_gather(image_low, "member", axis=0, tiled=True)
    members = group.shape[0]
    own_rows = lax.axis_index("member") * pairs + jnp.arange(pairs, dtype=jnp.int32)
    matched = (jnp.arange(members, dtype=jnp.int32)[:, None] == own_rows[None, :]).astype(
        jnp.float32
    )
    image_acc = jnp.zeros((members, width), jnp.float32)
    text_acc = jnp.zeros((pairs, width), jnp.float32)
    loss_acc = jnp.zeros((pairs,), jnp.float32)
    for step in range(STEPS):
        if step > 0:
            current = shifted(current, "blk", 1)
            text_acc, loss_acc = (
                shifted(text_acc.astype(jnp.bfloat16), "blk", 1).astype(text_acc.dtype),
                shifted(loss_acc.astype(jnp.bfloat16), "blk", 1).astype(loss_acc.dtype),
            )
        logits = (
            temper
            * lax.dot_general(
                group, current, (((1,), (1,)), ((), ())), preferred_element_type=jnp.float32
            )
            + offset
        )
        probs = jax.nn.sigmoid(logits)
        pair_loss = jax.nn.softplus(logits)
        if step == 0:
            probs = probs - matched
            pair_loss = pair_loss - matched * logits
        slope = probs.astype(jnp.bfloat16)
        image_acc = image_acc + jnp.dot(slope, current, preferred_element_type=jnp.float32)
        column_loss = jnp.sum(pair_loss, axis=0)
        text_acc = text_acc + text_term(slope, group)
        loss_acc = loss_acc + column_loss
    text_acc, loss_acc = (
        shifted(text_acc.astype(jnp.bfloat16), "blk", 1 - STEPS).astype(text_acc.dtype),
        shifted(loss_acc.astype(jnp.bfloat16), "blk", 1 - STEPS).astype(loss_acc.dtype),
    )
    image_sum = lax.psum_scatter(
        image_acc.astype(jnp.bfloat16), "member", scatter_dimension=0, tiled=True
    ).astype(jnp.float32)
    image_grad = chain_back(image_unit, image_inv, temper * image_sum)
    text_grad = chain_back(text_unit, text_inv, temper * text_acc)
    return (image_grad, text_grad, loss_acc / STEPS)


def solution(mesh):
    return jax.shard_map(
        on_device,
        mesh=mesh,
        in_specs=(P(("blk", "member"), None), P(("blk", "member"), None), P(), P()),
        out_specs=(P(("blk", "member"), None), P(("blk", "member"), None), P(("blk", "member"))),
        check_vma=False,
    )
```

profile of v0, /device:TPU:1, one launch (start us, length us, event | category | flops | bytes accessed | tf_op | source)
XLA Modules:
  0.0 230.0 jit_solution(14817190017735480780)
XLA Ops:
  7.2 1.1 fusion.18
  8.3 1.8 fusion.14
  12.4 4.6 %collective-permute-start = (bf16[128,1152]{1,0:T(8,128)(2,1)S(1)}, bf16[128,1152]{1,0:T(8,128)(2,1)S(1)}, u32[]{:S(2)}, u32[]{:S(2)}) collective-permute-start(bf16[128,1152]{1,0:T(8,128)(2,1)S(1)} %fusion.11), channel_id=1, source_target_pairs={{504,0},{0,8},{8,16},{16,24},{24,32},{32,40},{40,48},{48,56},{56,6... | collective-permute-start | bytes 884744 | tf_op jit(solution)/shard_map/ppermute | solution.py:12
  17.0 5.3 %collective-permute-done = bf16[128,1152]{1,0:T(8,128)(2,1)S(1)} collective-permute-done((bf16[128,1152]{1,0:T(8,128)(2,1)S(1)}, bf16[128,1152]{1,0:T(8,128)(2,1)S(1)}, u32[]{:S(2)}, u32[]{:S(2)}) %collective-permute-start) | collective-permute-done | bytes 294944 | tf_op jit(solution)/shard_map/ppermute | solution.py:12
  22.3 2.8 %collective-permute-start.1 = (bf16[128,1152]{1,0:T(8,128)(2,1)S(1)}, bf16[128,1152]{1,0:T(8,128)(2,1)S(1)}, u32[]{:S(2)}, u32[]{:S(2)}) collective-permute-start(bf16[128,1152]{1,0:T(8,128)(2,1)S(1)} %collective-permute-done), channel_id=1, source_target_pairs={{504,0},{0,8},{8,16},{16,24},{24,32},{32,40},{40,48},{48,56},{56,6... | collective-permute-start | bytes 884744 | tf_op jit(solution)/shard_map/ppermute | solution.py:12
  25.0 8.1 %collective-permute-done.1 = bf16[128,1152]{1,0:T(8,128)(2,1)S(1)} collective-permute-done((bf16[128,1152]{1,0:T(8,128)(2,1)S(1)}, bf16[128,1152]{1,0:T(8,128)(2,1)S(1)}, u32[]{:S(2)}, u32[]{:S(2)}) %collective-permute-start.1) | collective-permute-done | bytes 294944 | tf_op jit(solution)/shard_map/ppermute | solution.py:12
  33.1 1.9 collective-permute-start.2
  35.0 8.3 %collective-permute-done.2 = bf16[128,1152]{1,0:T(8,128)(2,1)S(1)} collective-permute-done((bf16[128,1152]{1,0:T(8,128)(2,1)S(1)}, bf16[128,1152]{1,0:T(8,128)(2,1)S(1)}, u32[]{:S(2)}, u32[]{:S(2)}) %collective-permute-start.2) | collective-permute-done | bytes 294944 | tf_op jit(solution)/shard_map/ppermute | solution.py:12
  43.4 2.9 %collective-permute-start.3 = (bf16[128,1152]{1,0:T(8,128)(2,1)S(1)}, bf16[128,1152]{1,0:T(8,128)(2,1)S(1)}, u32[]{:S(2)}, u32[]{:S(2)}) collective-permute-start(bf16[128,1152]{1,0:T(8,128)(2,1)S(1)} %collective-permute-done.2), channel_id=1, source_target_pairs={{504,0},{0,8},{8,16},{16,24},{24,32},{32,40},{40,48},{48,56},{56,6... | collective-permute-start | bytes 884744 | tf_op jit(solution)/shard_map/ppermute | solution.py:12
  46.2 7.3 %collective-permute-done.3 = bf16[128,1152]{1,0:T(8,128)(2,1)S(1)} collective-permute-done((bf16[128,1152]{1,0:T(8,128)(2,1)S(1)}, bf16[128,1152]{1,0:T(8,128)(2,1)S(1)}, u32[]{:S(2)}, u32[]{:S(2)}) %collective-permute-start.3) | collective-permute-done | bytes 294944 | tf_op jit(solution)/shard_map/ppermute | solution.py:12
  53.5 1.9 collective-permute-start.4
  55.4 8.2 %collective-permute-done.4 = bf16[128,1152]{1,0:T(8,128)(2,1)S(1)} collective-permute-done((bf16[128,1152]{1,0:T(8,128)(2,1)S(1)}, bf16[128,1152]{1,0:T(8,128)(2,1)S(1)}, u32[]{:S(2)}, u32[]{:S(2)}) %collective-permute-start.4) | collective-permute-done | bytes 294944 | tf_op jit(solution)/shard_map/ppermute | solution.py:12
  63.6 1.9 collective-permute-start.5
  66.9 7.9 %collective-permute-done.5 = bf16[128,1152]{1,0:T(8,128)(2,1)} collective-permute-done((bf16[128,1152]{1,0:T(8,128)(2,1)S(1)}, bf16[128,1152]{1,0:T(8,128)(2,1)}, u32[]{:S(2)}, u32[]{:S(2)}) %collective-permute-start.5) | collective-permute-done | bytes 294944 | tf_op jit(solution)/shard_map/ppermute | solution.py:12
  74.9 4.5 %collective-permute-start.6 = (bf16[128,1152]{1,0:T(8,128)(2,1)}, bf16[128,1152]{1,0:T(8,128)(2,1)}, u32[]{:S(2)}, u32[]{:S(2)}) collective-permute-start(bf16[128,1152]{1,0:T(8,128)(2,1)} %collective-permute-done.5), channel_id=1, source_target_pairs={{504,0},{0,8},{8,16},{16,24},{24,32},{32,40},{40,48},{48,56},{56,6... | collective-permute-start | bytes 884744 | tf_op jit(solution)/shard_map/ppermute | solution.py:12
  79.3 13.2 %all-gather.2.cloned.1.call-done = bf16[1024,1152]{1,0:T(8,128)(2,1)} async-done(((bf16[128,1152]{1,0:T(8,128)(2,1)}), bf16[1024,1152]{1,0:T(8,128)(2,1)}) %all-gather.2.cloned.1.call-update) | async-done | bytes 2359312 | tf_op jit(solution)/shard_map/all_gather | solution.py:40
  92.5 2.7 %fusion.24 = (bf16[128]{0:T(256)(128)(2,1)S(1)}, f32[1024,128]{1,0:T(8,128)S(1)}) fusion(s32[128]{0:T(128)S(1)} %iota_add_fusion, f32[]{:T(128)} %bitcast.34, bf16[1024,1152]{1,0:T(8,128)(2,1)} %all-gather.2.cloned.1.call-done, bf16[128,1152]{1,0:T(8,128)(2,1)S(1)} %fusion.11, f32[]{:T(128)} %bitcast), kind=kOutput, calls=%fused_computation.61 | convolution fusion | flops 303562624 | bytes 3179272 | tf_op jit(solution)/shard_map/dot_general | solution.py:58
  95.3 6.7 %collective-permute-start.15 = (bf16[128]{0:T(256)(128)(2,1)S(1)}, bf16[128]{0:T(256)(128)(2,1)S(1)}, u32[]{:S(2)}, u32[]{:S(2)}) collective-permute-start(bf16[128]{0:T(256)(128)(2,1)S(1)} %get-tuple-element.17), channel_id=1, source_target_pairs={{504,0},{0,8},{8,16},{16,24},{24,32},{32,40},{40,48},{48,56},{56,6... | collective-permute-start | bytes 776 | tf_op jit(solution)/shard_map/ppermute | solution.py:12
  103.7 1.3 convolution_convert_fusion
  105.0 2.1 collective-permute-start.7
  107.1 2.0 fusion.30
  114.1 2.0 fusion.31
  121.0 1.7 convolution_add_fusion.1
  122.7 3.2 %fusion = bf16[1024,1152]{1,0:T(8,128)(2,1)} fusion(f32[1024,1152]{1,0:T(8,128)S(1)} %convolution_add_fusion.1, bf16[128,1152]{1,0:T(8,128)(2,1)} %collective-permute-done.6, f32[1024,128]{1,0:T(8,128)S(1)} %get-tuple-element.4), kind=kOutput, calls=%fused_computation.7 | convolution fusion | flops 304873472 | bytes 7897088 | tf_op jit(solution)/shard_map/dot_general | solution.py:69
  125.9 2.4 %add_convert_fusion.6 = bf16[128,1152]{1,0:T(8,128)(2,1)S(1)} fusion(bf16[128,1152]{1,0:T(8,128)(2,1)} %collective-permute-done.7, bf16[1024,1152]{1,0:T(8,128)(2,1)} %all-gather.2.cloned.1.call-done, f32[1024,128]{1,0:T(8,128)S(1)} %get-tuple-element.16), kind=kOutput, calls=%fused_computation.58 | convolution fusion | flops 302956544 | bytes 3473408 | tf_op jit(solution)/shard_map/dot_general | solution.py:26
  128.3 1.9 collective-permute-start.8
  130.8 2.1 collective-permute-start.16
  133.9 4.4 %collective-permute-start.9 = (bf16[128,1152]{1,0:T(8,128)(2,1)S(1)}, bf16[128,1152]{1,0:T(8,128)(2,1)S(1)}, u32[]{:S(2)}, u32[]{:S(2)}) collective-permute-start(bf16[128,1152]{1,0:T(8,128)(2,1)S(1)} %add_convert_fusion.5), channel_id=1, source_target_pairs={{504,0},{0,8},{8,16},{16,24},{24,32},{32,40},{40,48},{48,56},{56,6... | collective-permute-start | bytes 884744 | tf_op jit(solution)/shard_map/ppermute | solution.py:12
  138.9 1.9 collective-permute-start.17
  140.9 1.4 collective-permute-done.9
  142.3 4.4 %collective-permute-start.10 = (bf16[128,1152]{1,0:T(8,128)(2,1)S(1)}, bf16[128,1152]{1,0:T(8,128)(2,1)S(1)}, u32[]{:S(2)}, u32[]{:S(2)}) collective-permute-start(bf16[128,1152]{1,0:T(8,128)(2,1)S(1)} %add_convert_fusion.4), channel_id=1, source_target_pairs={{504,0},{0,8},{8,16},{16,24},{24,32},{32,40},{40,48},{48,56},{56,6... | collective-permute-start | bytes 884744 | tf_op jit(solution)/shard_map/ppermute | solution.py:12
  147.3 1.9 collective-permute-start.18
  149.2 3.1 %collective-permute-done.10 = bf16[128,1152]{1,0:T(8,128)(2,1)S(1)} collective-permute-done((bf16[128,1152]{1,0:T(8,128)(2,1)S(1)}, bf16[128,1152]{1,0:T(8,128)(2,1)S(1)}, u32[]{:S(2)}, u32[]{:S(2)}) %collective-permute-start.10) | collective-permute-done | bytes 294944 | tf_op jit(solution)/shard_map/ppermute | solution.py:12
  152.4 2.4 %collective-permute-start.11 = (bf16[128,1152]{1,0:T(8,128)(2,1)S(1)}, bf16[128,1152]{1,0:T(8,128)(2,1)S(1)}, u32[]{:S(2)}, u32[]{:S(2)}) collective-permute-start(bf16[128,1152]{1,0:T(8,128)(2,1)S(1)} %add_convert_fusion.3), channel_id=1, source_target_pairs={{504,0},{0,8},{8,16},{16,24},{24,32},{32,40},{40,48},{48,56},{56,6... | collective-permute-start | bytes 884744 | tf_op jit(solution)/shard_map/ppermute | solution.py:12
  155.4 1.9 collective-permute-start.19
  157.3 5.3 %collective-permute-done.11 = bf16[128,1152]{1,0:T(8,128)(2,1)S(1)} collective-permute-done((bf16[128,1152]{1,0:T(8,128)(2,1)S(1)}, bf16[128,1152]{1,0:T(8,128)(2,1)S(1)}, u32[]{:S(2)}, u32[]{:S(2)}) %collective-permute-start.11) | collective-permute-done | bytes 294944 | tf_op jit(solution)/shard_map/ppermute | solution.py:12
  162.7 2.7 %collective-permute-start.12 = (bf16[128,1152]{1,0:T(8,128)(2,1)S(1)}, bf16[128,1152]{1,0:T(8,128)(2,1)S(1)}, u32[]{:S(2)}, u32[]{:S(2)}) collective-permute-start(bf16[128,1152]{1,0:T(8,128)(2,1)S(1)} %add_convert_fusion.2), channel_id=1, source_target_pairs={{504,0},{0,8},{8,16},{16,24},{24,32},{32,40},{40,48},{48,56},{56,6... | collective-permute-start | bytes 884744 | tf_op jit(solution)/shard_map/ppermute | solution.py:12
  166.0 1.9 collective-permute-start.20
  167.9 5.0 %collective-permute-done.12 = bf16[128,1152]{1,0:T(8,128)(2,1)S(1)} collective-permute-done((bf16[128,1152]{1,0:T(8,128)(2,1)S(1)}, bf16[128,1152]{1,0:T(8,128)(2,1)S(1)}, u32[]{:S(2)}, u32[]{:S(2)}) %collective-permute-start.12) | collective-permute-done | bytes 294944 | tf_op jit(solution)/shard_map/ppermute | solution.py:12
  173.0 2.1 collective-permute-start.13
  175.7 2.1 collective-permute-start.21
  177.8 5.6 %collective-permute-done.13 = bf16[128,1152]{1,0:T(8,128)(2,1)S(1)} collective-permute-done((bf16[128,1152]{1,0:T(8,128)(2,1)S(1)}, bf16[128,1152]{1,0:T(8,128)(2,1)S(1)}, u32[]{:S(2)}, u32[]{:S(2)}) %collective-permute-start.13) | collective-permute-done | bytes 294944 | tf_op jit(solution)/shard_map/ppermute | solution.py:12
  183.5 5.4 %collective-permute-start.14 = (bf16[128,1152]{1,0:T(8,128)(2,1)S(1)}, bf16[128,1152]{1,0:T(8,128)(2,1)S(1)}, u32[]{:S(2)}, u32[]{:S(2)}) collective-permute-start(bf16[128,1152]{1,0:T(8,128)(2,1)S(1)} %add_convert_fusion), channel_id=1, source_target_pairs={{56,0},{64,8},{72,16},{80,24},{88,32},{96,40},{104,48},{112,56},{1... | collective-permute-start | bytes 884744 | tf_op jit(solution)/shard_map/ppermute | solution.py:12
  188.9 2.9 %collective-permute-start.22 = (bf16[128]{0:T(256)(128)(2,1)S(1)}, bf16[128]{0:T(256)(128)(2,1)S(1)}, u32[]{:S(2)}, u32[]{:S(2)}) collective-permute-start(bf16[128]{0:T(256)(128)(2,1)S(1)} %add_convert_fusion.7), channel_id=1, source_target_pairs={{56,0},{64,8},{72,16},{80,24},{88,32},{96,40},{104,48},{112,56},{1... | collective-permute-start | bytes 776 | tf_op jit(solution)/shard_map/ppermute | solution.py:12
  191.8 8.7 %collective-permute-done.22 = bf16[128]{0:T(256)(128)(2,1)S(1)} collective-permute-done((bf16[128]{0:T(256)(128)(2,1)S(1)}, bf16[128]{0:T(256)(128)(2,1)S(1)}, u32[]{:S(2)}, u32[]{:S(2)}) %collective-permute-start.22) | collective-permute-done | bytes 288 | tf_op jit(solution)/shard_map/ppermute | solution.py:12
  202.3 17.6 %reduce-scatter.2.cloned.1.call-done = bf16[128,1152]{1,0:T(8,128)(2,1)} async-done(((bf16[1024,1152]{1,0:T(8,128)(2,1)}), bf16[128,1152]{1,0:T(8,128)(2,1)}) %reduce-scatter.2.cloned.1.call-update) | async-done | bytes 294928 | tf_op jit(solution)/shard_map/reduce_scatter | solution.py:77
  219.9 1.2 fusion.15
  221.1 2.0 fusion.17
  (81 shorter events, 20.3 us)
Async XLA Ops:
  7.2 85.3 %all-gather.2.cloned.1.call-start = ((), (), s32[]{:S(2)}) async-start(), calls=%async_computation.1 | async-start | bytes 2654208 | tf_op jit(solution)/shard_map/all_gather | solution.py:40
  10.1 209.8 %reduce-scatter.2.cloned.1.call-start = ((), (), s32[]{:S(2)}) async-start(), calls=%async_computation.2 | async-start | bytes 2654208 | tf_op jit(solution)/shard_map/reduce_scatter | solution.py:77
  12.4 9.9 %collective-permute-start = (bf16[128,1152]{1,0:T(8,128)(2,1)S(1)}, bf16[128,1152]{1,0:T(8,128)(2,1)S(1)}, u32[]{:S(2)}, u32[]{:S(2)}) collective-permute-start(bf16[128,1152]{1,0:T(8,128)(2,1)S(1)} %fusion.11), channel_id=1, source_target_pairs={{504,0},{0,8},{8,16},{16,24},{24,32},{32,40},{40,48},{48,56},{56,6... | collective-permute-start | bytes 884744 | tf_op jit(solution)/shard_map/ppermute | solution.py:12
  22.3 10.9 %collective-permute-start.1 = (bf16[128,1152]{1,0:T(8,128)(2,1)S(1)}, bf16[128,1152]{1,0:T(8,128)(2,1)S(1)}, u32[]{:S(2)}, u32[]{:S(2)}) collective-permute-start(bf16[128,1152]{1,0:T(8,128)(2,1)S(1)} %collective-permute-done), channel_id=1, source_target_pairs={{504,0},{0,8},{8,16},{16,24},{24,32},{32,40},{40,48},{48,56},{56,6... | collective-permute-start | bytes 884744 | tf_op jit(solution)/shard_map/ppermute | solution.py:12
  33.1 79.0 %copy-start.4 = (bf16[128,1152]{1,0:T(8,128)(2,1)}, bf16[128,1152]{1,0:T(8,128)(2,1)S(1)}, u32[]{:S(2)}) copy-start(bf16[128,1152]{1,0:T(8,128)(2,1)S(1)} %collective-permute-done.1) | copy-start | bytes 884740
  33.1 10.2 %collective-permute-start.2 = (bf16[128,1152]{1,0:T(8,128)(2,1)S(1)}, bf16[128,1152]{1,0:T(8,128)(2,1)S(1)}, u32[]{:S(2)}, u32[]{:S(2)}) collective-permute-start(bf16[128,1152]{1,0:T(8,128)(2,1)S(1)} %collective-permute-done.1), channel_id=1, source_target_pairs={{504,0},{0,8},{8,16},{16,24},{24,32},{32,40},{40,48},{48,56},{56,6... | collective-permute-start | bytes 884744 | tf_op jit(solution)/shard_map/ppermute | solution.py:12
  43.4 67.7 %copy-start.6 = (bf16[128,1152]{1,0:T(8,128)(2,1)}, bf16[128,1152]{1,0:T(8,128)(2,1)S(1)}, u32[]{:S(2)}) copy-start(bf16[128,1152]{1,0:T(8,128)(2,1)S(1)} %collective-permute-done.2) | copy-start | bytes 884740
  43.4 10.1 %collective-permute-start.3 = (bf16[128,1152]{1,0:T(8,128)(2,1)S(1)}, bf16[128,1152]{1,0:T(8,128)(2,1)S(1)}, u32[]{:S(2)}, u32[]{:S(2)}) collective-permute-start(bf16[128,1152]{1,0:T(8,128)(2,1)S(1)} %collective-permute-done.2), channel_id=1, source_target_pairs={{504,0},{0,8},{8,16},{16,24},{24,32},{32,40},{40,48},{48,56},{56,6... | collective-permute-start | bytes 884744 | tf_op jit(solution)/shard_map/ppermute | solution.py:12
  53.5 56.6 %copy-start.8 = (bf16[128,1152]{1,0:T(8,128)(2,1)}, bf16[128,1152]{1,0:T(8,128)(2,1)S(1)}, u32[]{:S(2)}) copy-start(bf16[128,1152]{1,0:T(8,128)(2,1)S(1)} %collective-permute-done.3) | copy-start | bytes 884740
  53.5 10.1 %collective-permute-start.4 = (bf16[128,1152]{1,0:T(8,128)(2,1)S(1)}, bf16[128,1152]{1,0:T(8,128)(2,1)S(1)}, u32[]{:S(2)}, u32[]{:S(2)}) collective-permute-start(bf16[128,1152]{1,0:T(8,128)(2,1)S(1)} %collective-permute-done.3), channel_id=1, source_target_pairs={{504,0},{0,8},{8,16},{16,24},{24,32},{32,40},{40,48},{48,56},{56,6... | collective-permute-start | bytes 884744 | tf_op jit(solution)/shard_map/ppermute | solution.py:12
  63.6 45.4 %copy-start.10 = (bf16[128,1152]{1,0:T(8,128)(2,1)}, bf16[128,1152]{1,0:T(8,128)(2,1)S(1)}, u32[]{:S(2)}) copy-start(bf16[128,1152]{1,0:T(8,128)(2,1)S(1)} %collective-permute-done.4) | copy-start | bytes 884740
  63.6 11.2 %collective-permute-start.5 = (bf16[128,1152]{1,0:T(8,128)(2,1)S(1)}, bf16[128,1152]{1,0:T(8,128)(2,1)}, u32[]{:S(2)}, u32[]{:S(2)}) collective-permute-start(bf16[128,1152]{1,0:T(8,128)(2,1)S(1)} %collective-permute-done.4), channel_id=1, source_target_pairs={{504,0},{0,8},{8,16},{16,24},{24,32},{32,40},{40,48},{48,56},{56,6... | collective-permute-start | bytes 884744 | tf_op jit(solution)/shard_map/ppermute | solution.py:12
  74.9 39.3 %collective-permute-start.6 = (bf16[128,1152]{1,0:T(8,128)(2,1)}, bf16[128,1152]{1,0:T(8,128)(2,1)}, u32[]{:S(2)}, u32[]{:S(2)}) collective-permute-start(bf16[128,1152]{1,0:T(8,128)(2,1)} %collective-permute-done.5), channel_id=1, source_target_pairs={{504,0},{0,8},{8,16},{16,24},{24,32},{32,40},{40,48},{48,56},{56,6... | collective-permute-start | bytes 884744 | tf_op jit(solution)/shard_map/ppermute | solution.py:12
  95.3 35.6 %collective-permute-start.15 = (bf16[128]{0:T(256)(128)(2,1)S(1)}, bf16[128]{0:T(256)(128)(2,1)S(1)}, u32[]{:S(2)}, u32[]{:S(2)}) collective-permute-start(bf16[128]{0:T(256)(128)(2,1)S(1)} %get-tuple-element.17), channel_id=1, source_target_pairs={{504,0},{0,8},{8,16},{16,24},{24,32},{32,40},{40,48},{48,56},{56,6... | collective-permute-start | bytes 776 | tf_op jit(solution)/shard_map/ppermute | solution.py:12
  102.0 1.7 copy-start.12
  105.0 20.9 %collective-permute-start.7 = (bf16[128,1152]{1,0:T(8,128)(2,1)}, bf16[128,1152]{1,0:T(8,128)(2,1)}, u32[]{:S(2)}, u32[]{:S(2)}) collective-permute-start(bf16[128,1152]{1,0:T(8,128)(2,1)} %convolution_convert_fusion), channel_id=1, source_target_pairs={{504,0},{0,8},{8,16},{16,24},{24,32},{32,40},{40,48},{48,56},{56,6... | collective-permute-start | bytes 884744 | tf_op jit(solution)/shard_map/ppermute | solution.py:12
  116.1 6.6 %copy-start.2 = (f32[1024,128]{1,0:T(8,128)}, f32[1024,128]{1,0:T(8,128)S(1)}, u32[]{:S(2)}) copy-start(f32[1024,128]{1,0:T(8,128)S(1)} %get-tuple-element.4) | copy-start | bytes 1572868
  116.1 1.2 copy-start.5
  117.3 1.0 copy-start.7
  118.2 1.0 copy-start.9
  119.2 1.0 copy-start.11
  125.9 4.3 %copy-start.13 = (bf16[1024,1152]{1,0:T(8,128)(2,1)S(1)}, bf16[1024,1152]{1,0:T(8,128)(2,1)}, u32[]{:S(2)}) copy-start(bf16[1024,1152]{1,0:T(8,128)(2,1)} %all-gather.2.cloned.1.call-done) | copy-start | bytes 7077892
  128.3 5.6 %collective-permute-start.8 = (bf16[128,1152]{1,0:T(8,128)(2,1)S(1)}, bf16[128,1152]{1,0:T(8,128)(2,1)S(1)}, u32[]{:S(2)}, u32[]{:S(2)}) collective-permute-start(bf16[128,1152]{1,0:T(8,128)(2,1)S(1)} %add_convert_fusion.6), channel_id=1, source_target_pairs={{504,0},{0,8},{8,16},{16,24},{24,32},{32,40},{40,48},{48,56},{56,6... | collective-permute-start | bytes 884744 | tf_op jit(solution)/shard_map/ppermute | solution.py:12
  130.8 8.1 %collective-permute-start.16 = (bf16[128]{0:T(256)(128)(2,1)S(1)}, bf16[128]{0:T(256)(128)(2,1)S(1)}, u32[]{:S(2)}, u32[]{:S(2)}) collective-permute-start(bf16[128]{0:T(256)(128)(2,1)S(1)} %add_convert_fusion.13), channel_id=1, source_target_pairs={{504,0},{0,8},{8,16},{16,24},{24,32},{32,40},{40,48},{48,56},{56,6... | collective-permute-start | bytes 776 | tf_op jit(solution)/shard_map/ppermute | solution.py:12
  133.9 8.3 %collective-permute-start.9 = (bf16[128,1152]{1,0:T(8,128)(2,1)S(1)}, bf16[128,1152]{1,0:T(8,128)(2,1)S(1)}, u32[]{:S(2)}, u32[]{:S(2)}) collective-permute-start(bf16[128,1152]{1,0:T(8,128)(2,1)S(1)} %add_convert_fusion.5), channel_id=1, source_target_pairs={{504,0},{0,8},{8,16},{16,24},{24,32},{32,40},{40,48},{48,56},{56,6... | collective-permute-start | bytes 884744 | tf_op jit(solution)/shard_map/ppermute | solution.py:12
  138.9 8.3 %collective-permute-start.17 = (bf16[128]{0:T(256)(128)(2,1)S(1)}, bf16[128]{0:T(256)(128)(2,1)S(1)}, u32[]{:S(2)}, u32[]{:S(2)}) collective-permute-start(bf16[128]{0:T(256)(128)(2,1)S(1)} %add_convert_fusion.12), channel_id=1, source_target_pairs={{504,0},{0,8},{8,16},{16,24},{24,32},{32,40},{40,48},{48,56},{56,6... | collective-permute-start | bytes 776 | tf_op jit(solution)/shard_map/ppermute | solution.py:12
  142.3 10.0 %collective-permute-start.10 = (bf16[128,1152]{1,0:T(8,128)(2,1)S(1)}, bf16[128,1152]{1,0:T(8,128)(2,1)S(1)}, u32[]{:S(2)}, u32[]{:S(2)}) collective-permute-start(bf16[128,1152]{1,0:T(8,128)(2,1)S(1)} %add_convert_fusion.4), channel_id=1, source_target_pairs={{504,0},{0,8},{8,16},{16,24},{24,32},{32,40},{40,48},{48,56},{56,6... | collective-permute-start | bytes 884744 | tf_op jit(solution)/shard_map/ppermute | solution.py:12
  147.3 8.1 %collective-permute-start.18 = (bf16[128]{0:T(256)(128)(2,1)S(1)}, bf16[128]{0:T(256)(128)(2,1)S(1)}, u32[]{:S(2)}, u32[]{:S(2)}) collective-permute-start(bf16[128]{0:T(256)(128)(2,1)S(1)} %add_convert_fusion.11), channel_id=1, source_target_pairs={{504,0},{0,8},{8,16},{16,24},{24,32},{32,40},{40,48},{48,56},{56,6... | collective-permute-start | bytes 776 | tf_op jit(solution)/shard_map/ppermute | solution.py:12
  152.4 10.2 %collective-permute-start.11 = (bf16[128,1152]{1,0:T(8,128)(2,1)S(1)}, bf16[128,1152]{1,0:T(8,128)(2,1)S(1)}, u32[]{:S(2)}, u32[]{:S(2)}) collective-permute-start(bf16[128,1152]{1,0:T(8,128)(2,1)S(1)} %add_convert_fusion.3), channel_id=1, source_target_pairs={{504,0},{0,8},{8,16},{16,24},{24,32},{32,40},{40,48},{48,56},{56,6... | collective-permute-start | bytes 884744 | tf_op jit(solution)/shard_map/ppermute | solution.py:12
  155.4 10.6 %collective-permute-start.19 = (bf16[128]{0:T(256)(128)(2,1)S(1)}, bf16[128]{0:T(256)(128)(2,1)S(1)}, u32[]{:S(2)}, u32[]{:S(2)}) collective-permute-start(bf16[128]{0:T(256)(128)(2,1)S(1)} %add_convert_fusion.10), channel_id=1, source_target_pairs={{504,0},{0,8},{8,16},{16,24},{24,32},{32,40},{40,48},{48,56},{56,6... | collective-permute-start | bytes 776 | tf_op jit(solution)/shard_map/ppermute | solution.py:12
  162.7 12.4 %copy-start.3 = (f32[1024,128]{1,0:T(8,128)S(1)}, f32[1024,128]{1,0:T(8,128)}, u32[]{:S(2)}) copy-start(f32[1024,128]{1,0:T(8,128)} %copy-done.2) | copy-start | bytes 1572868
  162.7 10.3 %collective-permute-start.12 = (bf16[128,1152]{1,0:T(8,128)(2,1)S(1)}, bf16[128,1152]{1,0:T(8,128)(2,1)S(1)}, u32[]{:S(2)}, u32[]{:S(2)}) collective-permute-start(bf16[128,1152]{1,0:T(8,128)(2,1)S(1)} %add_convert_fusion.2), channel_id=1, source_target_pairs={{504,0},{0,8},{8,16},{16,24},{24,32},{32,40},{40,48},{48,56},{56,6... | collective-permute-start | bytes 884744 | tf_op jit(solution)/shard_map/ppermute | solution.py:12
  166.0 9.7 %collective-permute-start.20 = (bf16[128]{0:T(256)(128)(2,1)S(1)}, bf16[128]{0:T(256)(128)(2,1)S(1)}, u32[]{:S(2)}, u32[]{:S(2)}) collective-permute-start(bf16[128]{0:T(256)(128)(2,1)S(1)} %add_convert_fusion.9), channel_id=1, source_target_pairs={{504,0},{0,8},{8,16},{16,24},{24,32},{32,40},{40,48},{48,56},{56,6... | collective-permute-start | bytes 776 | tf_op jit(solution)/shard_map/ppermute | solution.py:12
  173.0 28.0 %copy-start = (bf16[128,1152]{1,0:T(8,128)(2,1)S(1)}, bf16[128,1152]{1,0:T(8,128)(2,1)}, u32[]{:S(2)}) copy-start(bf16[128,1152]{1,0:T(8,128)(2,1)} %param.5) | copy-start | bytes 884740
  173.0 10.4 %collective-permute-start.13 = (bf16[128,1152]{1,0:T(8,128)(2,1)S(1)}, bf16[128,1152]{1,0:T(8,128)(2,1)S(1)}, u32[]{:S(2)}, u32[]{:S(2)}) collective-permute-start(bf16[128,1152]{1,0:T(8,128)(2,1)S(1)} %add_convert_fusion.1), channel_id=1, source_target_pairs={{504,0},{0,8},{8,16},{16,24},{24,32},{32,40},{40,48},{48,56},{56,6... | collective-permute-start | bytes 884744 | tf_op jit(solution)/shard_map/ppermute | solution.py:12
  175.7 44.3 %copy-start.1 = (bf16[128,1152]{1,0:T(8,128)(2,1)S(1)}, bf16[128,1152]{1,0:T(8,128)(2,1)}, u32[]{:S(2)}) copy-start(bf16[128,1152]{1,0:T(8,128)(2,1)} %param.4) | copy-start | bytes 884740
  175.7 13.2 %collective-permute-start.21 = (bf16[128]{0:T(256)(128)(2,1)S(1)}, bf16[128]{0:T(256)(128)(2,1)S(1)}, u32[]{:S(2)}, u32[]{:S(2)}) collective-permute-start(bf16[128]{0:T(256)(128)(2,1)S(1)} %add_convert_fusion.8), channel_id=1, source_target_pairs={{504,0},{0,8},{8,16},{16,24},{24,32},{32,40},{40,48},{48,56},{56,6... | collective-permute-start | bytes 776 | tf_op jit(solution)/shard_map/ppermute | solution.py:12
  183.5 17.5 %collective-permute-start.14 = (bf16[128,1152]{1,0:T(8,128)(2,1)S(1)}, bf16[128,1152]{1,0:T(8,128)(2,1)S(1)}, u32[]{:S(2)}, u32[]{:S(2)}) collective-permute-start(bf16[128,1152]{1,0:T(8,128)(2,1)S(1)} %add_convert_fusion), channel_id=1, source_target_pairs={{56,0},{64,8},{72,16},{80,24},{88,32},{96,40},{104,48},{112,56},{1... | collective-permute-start | bytes 884744 | tf_op jit(solution)/shard_map/ppermute | solution.py:12
  188.9 11.6 %collective-permute-start.22 = (bf16[128]{0:T(256)(128)(2,1)S(1)}, bf16[128]{0:T(256)(128)(2,1)S(1)}, u32[]{:S(2)}, u32[]{:S(2)}) collective-permute-start(bf16[128]{0:T(256)(128)(2,1)S(1)} %add_convert_fusion.7), channel_id=1, source_target_pairs={{56,0},{64,8},{72,16},{80,24},{88,32},{96,40},{104,48},{112,56},{1... | collective-permute-start | bytes 776 | tf_op jit(solution)/shard_map/ppermute | solution.py:12
Sparse Core Ops, SparseCore 0:
  11.8 80.7 all-gather.1
  126.0 93.8 reduce-scatter.1
where the time goes:
time: 231 us; the launch traced here: 230 us
  waiting for transfers between devices  106 us (46%)
  starting transfers between devices  67.4 us (29%)
  matrix products  28.5 us (12%)
  between operations  15.9 us (7%)
  other arithmetic  10.4 us (5%)
    ppermute x23, waiting for transfers between devices, shifted(): return lax.ppermute(block, axis, route)  75.2 us
    ppermute x23, starting transfers between devices, shifted(): return lax.ppermute(block, axis, route)  67.3 us
    reduce_scatter x1, waiting for transfers between devices, on_device(): lax.psum_scatter(image_acc.astype(jnp.bfloat16), 'member', scatter_dimens...  17.6 us
    all_gather x1, waiting for transfers between devices, on_device(): group = lax.all_gather(image_low, 'member', axis=0, tiled=True)  13.2 us
    dot_general x8, matrix products, on_device(): lax.dot_general(group, current, (((1,), (1,)), ((), ())), preferred_eleme...  11.7 us
    dot_general x8, matrix products, on_device(): jnp.dot(slope, current, preferred_element_type=jnp.float32)  9.59 us
    dot_general x8, matrix products, text_term(): lax.dot_general(slope, group, (((0,), (0,)), ((), ())), preferred_element...  7.12 us
  transfers between devices with their start and end apart: 25, of which 15 were waited for; matrix products, arithmetic and copies ran while one was open for 14% of the time, Pallas kernels for 0%

commit v1 on v0

v1 whole, which is shorter than its diff:
```python
import jax
import jax.numpy as jnp
from jax import lax
from jax.experimental import pallas as pl
from jax.experimental.pallas import tpu as pltpu
from jax.sharding import PartitionSpec as P

STEPS = 8
B = 128
HALF = B // 2
MESH = pl.DeviceIdType.MESH

OWN, XM, XP, Y, YXM, YXP, X2, YX2 = range(8)
T0B, T0A, T1A, T2A, T3A, T1B, T2B, T3B, RELAY = range(9)
G1A, G1B, G2A, G2B, G3A, G3B, GR, GS = range(8)


def normalized(ref):
    wide = ref[...].astype(jnp.float32)
    inverse = lax.rsqrt(jnp.sum(wide * wide, axis=-1, keepdims=True) + 1e-06)
    return wide * inverse, inverse


def chain_back(unit, inverse, upstream):
    return inverse * (upstream - unit * jnp.sum(unit * upstream, axis=-1, keepdims=True))


def kernel(
    images, texts, log_scale, bias, image_grad, text_grad, text_loss,
    img, txt, pg, tgr, loss, sp, rxh, rx, sg, rg, sl, rl, ssem, rsem,
):
    blk, member = lax.axis_index("blk"), lax.axis_index("member")
    n_blk, n_member = lax.axis_size("blk"), lax.axis_size("member")
    core = blk % 2
    y_lo = (blk // 2) % 2
    at_core = (blk + 1 - 2 * core, member)
    at_pair = (blk + 2 - 4 * y_lo, member)
    at_zp = ((blk + 4) % n_blk, member)
    at_zm = ((blk + n_blk - 4) % n_blk, member)
    at_xp = (blk, (member + 2) % n_member)
    at_xm = (blk, (member + n_member - 2) % n_member)
    at_y = (blk, member + 1 - 2 * (member % 2))

    barrier = pltpu.get_barrier_semaphore()
    partners = (at_core, at_pair, at_zp, at_zm, at_xp, at_xm, at_y)
    for device in partners:
        pl.semaphore_signal(barrier, inc=1, device_id=device, device_id_type=MESH)

    used = [0]
    sent = []

    def copies(src, src_row, dst, dst_row, rows, device, pieces=1, other=None):
        out = []
        step = rows // pieces
        for k in range(pieces):
            s = used[0]
            used[0] += 1
            made = [
                pltpu.make_async_remote_copy(
                    src_ref=a.at[pl.ds(r + k * step, step)],
                    dst_ref=dst.at[pl.ds(dst_row + k * step, step)],
                    send_sem=ssem.at[s],
                    recv_sem=rsem.at[s],
                    device_id=device,
                    device_id_type=MESH,
                )
                for a, r in [(src, src_row)] + ([other] if other else [])
            ]
            sent.append(made[0])
            out.append(made if other else made[0])
        return out

    f_xp = copies(img, OWN * B, img, XM * B, B, at_xp, 2)
    f_xm = copies(img, OWN * B, img, XP * B, B, at_xm, 2)
    f_y = copies(img, OWN * B, img, Y * B, B, at_y, 2)
    f_x2t = copies(img, XM * B, img, X2 * B, HALF, at_xp)
    f_x2b = copies(img, XP * B + HALF, img, X2 * B + HALF, HALF, at_xm)
    f_yxp = copies(img, Y * B, img, YXM * B, B, at_xp, 2)
    f_yxm = copies(img, Y * B, img, YXP * B, B, at_xm, 2)
    f_yx2t = copies(img, YXM * B, img, YX2 * B, HALF, at_xp)
    f_yx2b = copies(img, YXP * B + HALF, img, YX2 * B + HALF, HALF, at_xm)
    f_z1 = copies(txt, T0B * B, txt, T0A * B, B, at_zp, 2)
    f_z2 = copies(txt, T0A * B, txt, RELAY * B, B, at_zp, 2)
    f_c1a = copies(txt, T0A * B, txt, T1A * B, B, at_core)
    f_c1b = copies(txt, T0B * B, txt, T1B * B, B, at_core, 2, (txt, RELAY * B))
    f_p2a = copies(txt, T0A * B, txt, T2A * B, B, at_pair, 2)
    f_p2b = copies(txt, T0B * B, txt, T2B * B, B, at_pair, 2, (txt, RELAY * B))
    f_c3a = copies(txt, T2A * B, txt, T3A * B, B, at_core)
    f_c3b = copies(txt, T2B * B, txt, T3B * B, B, at_core)
    b_7t = copies(sp, YX2 * B, rxh, 0, HALF, at_xm)
    b_7b = copies(sp, YX2 * B + HALF, rxh, HALF, HALF, at_xp)
    b_6t = copies(sp, X2 * B, rxh, 2 * HALF, HALF, at_xm)
    b_6b = copies(sp, X2 * B + HALF, rxh, 3 * HALF, HALF, at_xp)
    b_4 = copies(sp, YXM * B, rx, 0 * B, B, at_xm, 2)
    b_5 = copies(sp, YXP * B, rx, 1 * B, B, at_xp, 2)
    b_1 = copies(sp, XM * B, rx, 2 * B, B, at_xm, 2)
    b_2 = copies(sp, XP * B, rx, 3 * B, B, at_xp, 2)
    b_3 = copies(sp, Y * B, rx, 4 * B, B, at_y, 2)
    b_c3a = copies(sg, G3A * B, rg, G3A * B, B, at_core)
    b_c3b = copies(sg, G3B * B, rg, G3B * B, B, at_core)
    b_c1 = copies(sg, G1A * B, rg, G1A * B, 2 * B, at_core)
    b_p2b = copies(sg, G2B * B, rg, G2B * B, B, at_pair, 2)
    b_p2a = copies(sg, G2A * B, rg, G2A * B, B, at_pair, 2)
    b_zr = copies(sg, GR * B, rg, GR * B, B, at_zm, 2)
    b_zs = copies(sg, GS * B, rg, GS * B, B, at_zm, 2)
    l_c = copies(sl, 0, rl, 0, 8, at_core)
    l_p = copies(sl, 8, rl, 8, 8, at_pair)
    l_zr = copies(sl, 16, rl, 16, 8, at_zm)
    l_zs = copies(sl, 24, rl, 24, 8, at_zm)

    def start(*lists):
        for group in lists:
            for c in group:
                c.start()

    def landed(*lists):
        for group in lists:
            for c in group:
                (c[0] if isinstance(c, list) else c).wait_recv()

    def start_choice(group, which):
        for c in group:
            c[which].start()

    temper = jnp.exp(jnp.full((1, B), log_scale[0], jnp.float32))
    offset = bias[0]

    unit, _ = normalized(images)
    img[pl.ds(OWN * B, B), :] = unit.astype(jnp.bfloat16)
    unit, _ = normalized(texts)
    txt[pl.ds(T0B * B, B), :] = unit.astype(jnp.bfloat16)

    pl.semaphore_wait(barrier, len(partners))

    start(f_y, f_xp, f_xm, f_z1)

    @pl.when(core == 0)
    def _():
        start_choice(f_c1b, 0)

    @pl.when(y_lo == 0)
    def _():
        start_choice(f_p2b, 0)

    pg[...] = jnp.zeros_like(pg)
    tgr[...] = jnp.zeros_like(tgr)
    loss[...] = jnp.zeros_like(loss)

    def tile(row, rows, first, blocks, diagonal=False):
        cols = blocks * B
        i = img[pl.ds(row, rows), :]
        t = txt[pl.ds(first * B, cols), :]
        scale = jnp.concatenate([temper] * blocks, axis=1)
        logits = (
            lax.dot_general(i, t, (((1,), (1,)), ((), ())), preferred_element_type=jnp.float32)
            * scale
            + offset
        )
        grown = jnp.exp(logits)
        slope = grown * pl.reciprocal(1.0 + grown, approx=True)
        part = rows
        while part > rows // 8:
            part //= 2
            grown = grown[:part] + grown[part:] + grown[:part] * grown[part:]
        logs = jnp.where(
            grown < 0.0078125,
            grown * (1.0 - grown * (0.5 - grown * (1.0 / 3.0))),
            jnp.log(1.0 + grown),
        )
        column = jnp.sum(logs, axis=0, keepdims=True)
        if diagonal:
            at_row = row + lax.broadcasted_iota(jnp.int32, (rows, cols), 0)
            at_col = first * B + lax.broadcasted_iota(jnp.int32, (rows, cols), 1)
            matched = jnp.logical_and(at_row == at_col, at_col < B)
            slope = slope - jnp.where(matched, 1.0, 0.0)
            column = column - jnp.sum(jnp.where(matched, logits, 0.0), axis=0, keepdims=True)
        for k in range(blocks):
            loss[pl.ds(first + k, 1), :] += column[:, k * B : (k + 1) * B]
        low = slope.astype(jnp.bfloat16)
        pg[pl.ds(row, rows), :] += jnp.dot(low, t, preferred_element_type=jnp.float32)
        tgr[pl.ds(first * B, cols), :] += lax.dot_general(
            low, i, (((0,), (0,)), ((), ())), preferred_element_type=jnp.float32
        )

    def tiles(first_slot, slots, first, blocks, diagonal=False):
        def body(k, carry):
            row = pl.multiple_of((first_slot + 2 * k) * B, 2 * B)
            tile(row, 2 * B, first, blocks, diagonal)
            return carry

        lax.fori_loop(0, slots // 2, body, 0)

    landed(f_y)
    start(f_yxp, f_yxm)
    landed(f_xp, f_xm)
    start(f_x2t, f_x2b)
    landed(f_z1)
    start(f_z2, f_p2a, f_c1a)
    tiles(OWN, 4, T0B, 2, diagonal=True)
    landed(f_p2a)
    start(f_c3a)
    landed(f_z2)

    @pl.when(core == 1)
    def _():
        start_choice(f_c1b, 1)

    @pl.when(y_lo == 1)
    def _():
        start_choice(f_p2b, 1)

    landed(f_c1a, f_c3a, f_c1b)
    landed(f_yxp, f_yxm)
    start(f_yx2t, f_yx2b)
    tiles(OWN, 4, T1A, 4)
    tiles(YXM, 2, T0B, 6)
    landed(f_p2b)
    start(f_c3b)
    landed(f_c3b, f_x2t, f_x2b, f_yx2t, f_yx2b)
    tiles(X2, 2, T0B, 8)

    def stage(slot):
        sp[pl.ds(slot * B, B), :] = pg[pl.ds(slot * B, B), :].astype(jnp.bfloat16)

    stage(YX2)
    start(b_7t, b_7b)
    stage(X2)
    start(b_6t, b_6b)
    tiles(OWN, 6, T2B, 2)

    def text_sum(slot):
        return tgr[pl.ds(slot * B, B), :]

    def put(slot, value):
        sg[pl.ds(slot * B, B), :] = value.astype(jnp.bfloat16)

    def got(slot):
        return rg[pl.ds(slot * B, B), :].astype(jnp.float32)

    put(G3B, text_sum(T3B))
    start(b_c3b)
    put(G3A, text_sum(T3A))
    start(b_c3a)
    sl[pl.ds(0, 8), :] = loss[...]
    start(l_c)

    def pass_on(slot, top, half):
        add = HALF * half
        mine = pg[pl.ds(slot * B + (0 if top else HALF), HALF), :]
        total = mine + rxh[pl.ds(add, HALF), :].astype(jnp.float32)
        rest = slot * B + (HALF if top else 0)
        sp[pl.ds(rest, HALF), :] = pg[pl.ds(rest, HALF), :].astype(jnp.bfloat16)
        sp[pl.ds(slot * B + (0 if top else HALF), HALF), :] = total.astype(jnp.bfloat16)

    landed(b_7t, b_7b)
    pass_on(YXM, True, 0)
    start(b_4)
    pass_on(YXP, False, 1)
    start(b_5)

    landed(b_c3b)
    put(G2B, text_sum(T2B) + got(G3B))
    start(b_p2b)
    landed(b_c3a)
    put(G2A, text_sum(T2A) + got(G3A))
    start(b_p2a)
    put(G1A, text_sum(T1A))
    put(G1B, text_sum(T1B))
    start(b_c1)
    landed(l_c)
    loss_2a = loss[pl.ds(T2A, 1), :] + rl[pl.ds(T3A, 1), :]
    loss_2b = loss[pl.ds(T2B, 1), :] + rl[pl.ds(T3B, 1), :]
    sl[pl.ds(8, 8), :] = jnp.concatenate([loss_2a, loss_2b] * 4, axis=0)
    start(l_p)

    landed(b_6t, b_6b)
    pass_on(XM, True, 2)
    start(b_1)
    pass_on(XP, False, 3)
    start(b_2)

    odd = core.astype(jnp.float32)
    high = y_lo.astype(jnp.float32)
    landed(b_c1, b_p2b)
    put(GR, got(G1B) * odd + got(G2B) * high)
    start(b_zr)
    landed(l_p)
    sl[pl.ds(16, 8), :] = jnp.broadcast_to(
        rl[pl.ds(T1B, 1), :] * odd + rl[pl.ds(9, 1), :] * high, (8, B)
    )
    start(l_zr)

    landed(b_4, b_5)
    sp[pl.ds(Y * B, B), :] = (
        pg[pl.ds(Y * B, B), :]
        + rx[pl.ds(0 * B, B), :].astype(jnp.float32)
        + rx[pl.ds(1 * B, B), :].astype(jnp.float32)
    ).astype(jnp.bfloat16)
    start(b_3)

    landed(b_p2a)
    landed(b_zr)
    put(GS, text_sum(T0A) + got(G1A) + got(G2A) + got(GR))
    start(b_zs)
    landed(l_zr)
    sl[pl.ds(24, 8), :] = jnp.broadcast_to(
        loss[pl.ds(T0A, 1), :] + rl[pl.ds(T1A, 1), :] + rl[pl.ds(8, 1), :] + rl[pl.ds(16, 1), :], (8, B)
    )
    start(l_zs)

    wide_temper = jnp.concatenate([temper] * (images.shape[1] // B), axis=1)

    landed(b_1, b_2, b_3)
    image_sum = (
        pg[pl.ds(OWN * B, B), :]
        + rx[pl.ds(2 * B, B), :].astype(jnp.float32)
        + rx[pl.ds(3 * B, B), :].astype(jnp.float32)
        + rx[pl.ds(4 * B, B), :].astype(jnp.float32)
    )
    unit, inverse = normalized(images)
    image_grad[...] = chain_back(unit, inverse, wide_temper * image_sum)

    landed(b_zs, l_zs)
    own_sum = (
        text_sum(T0B) + got(G1B) * (1.0 - odd) + got(G2B) * (1.0 - high) + got(GS)
    )
    unit, inverse = normalized(texts)
    text_grad[...] = chain_back(unit, inverse, wide_temper * own_sum)
    text_loss[...] = (
        loss[pl.ds(T0B, 1), :]
        + rl[pl.ds(T1B, 1), :] * (1.0 - odd)
        + rl[pl.ds(9, 1), :] * (1.0 - high)
        + rl[pl.ds(24, 1), :]
    ) * (1.0 / STEPS)
    for c in sent:
        c.wait_send()


SEMS = 80


def on_device(images, texts, log_scale, bias):
    width = images.shape[1]
    rows = lambda n, dtype: pltpu.VMEM((n, width), dtype)
    vmem = pl.BlockSpec(memory_space=pltpu.VMEM)
    smem = pl.BlockSpec(memory_space=pltpu.SMEM)
    image_grad, text_grad, text_loss = pl.pallas_call(
        kernel,
        out_shape=(
            jax.ShapeDtypeStruct((B, width), jnp.float32),
            jax.ShapeDtypeStruct((B, width), jnp.float32),
            jax.ShapeDtypeStruct((1, B), jnp.float32),
        ),
        in_specs=[vmem, vmem, smem, smem],
        out_specs=(vmem, vmem, vmem),
        scratch_shapes=[
            rows(8 * B, jnp.bfloat16),
            rows(9 * B, jnp.bfloat16),
            rows(8 * B, jnp.float32),
            rows(8 * B, jnp.float32),
            pltpu.VMEM((8, B), jnp.float32),
            rows(8 * B, jnp.bfloat16),
            rows(4 * HALF, jnp.bfloat16),
            rows(5 * B, jnp.bfloat16),
            rows(8 * B, jnp.bfloat16),
            rows(8 * B, jnp.bfloat16),
            pltpu.VMEM((32, B), jnp.float32),
            pltpu.VMEM((32, B), jnp.float32),
            pltpu.SemaphoreType.DMA((SEMS,)),
            pltpu.SemaphoreType.DMA((SEMS,)),
        ],
        compiler_params=pltpu.CompilerParams(
            collective_id=0, has_side_effects=True, vmem_limit_bytes=52 << 20
        ),
        name="window",
    )(images, texts, log_scale, bias)
    return image_grad, text_grad, text_loss.reshape(B)


def solution(mesh):
    return jax.shard_map(
        on_device,
        mesh=mesh,
        in_specs=(P(("blk", "member"), None), P(("blk", "member"), None), P(), P()),
        out_specs=(P(("blk", "member"), None), P(("blk", "member"), None), P(("blk", "member"))),
        check_vma=False,
    )
```

time: 231 us -> 79.6 us (0.34)
  waiting for transfers between devices: 106 us -> 0 us
  Pallas kernels: 0 us -> 73.1 us
  starting transfers between devices: 67.4 us -> 0 us
  matrix products: 28.5 us -> 0 us
  between operations: 15.9 us -> 1.94 us
  other arithmetic: 10.4 us -> 0 us
    ppermute x23 -> x0, waiting for transfers between devices: 75.2 us -> none  [shifted(): return lax.ppermute(block, axis, route)]
    pallas_call x0 -> x1, Pallas kernels: none -> 73.1 us  [on_device(): pl.pallas_call(kernel, out_shape=(jax.ShapeDtypeStruct((B, width), jnp.fl...]
    ppermute x23 -> x0, starting transfers between devices: 67.3 us -> none  [shifted(): return lax.ppermute(block, axis, route)]
    dot_general x24 -> x0, matrix products: 28.5 us -> none  [the longest x8 11.7 us: on_device(): lax.dot_general(group, current, (((1,), (1,)), ((), ())), preferred_eleme...]
    reduce_scatter x1 -> x0, waiting for transfers between devices: 17.6 us -> none  [on_device(): lax.psum_scatter(image_acc.astype(jnp.bfloat16), 'member', scatter_dimens...]
    all_gather x1 -> x0, waiting for transfers between devices: 13.2 us -> none  [on_device(): group = lax.all_gather(image_low, 'member', axis=0, tiled=True)]
    reduce_sum x4 -> x0, other arithmetic: 3.62 us -> none  [the longest x2 2.21 us: normalize(): inverse = lax.rsqrt(jnp.sum(wide * wide, axis=-1, keepdims=True) + 1e-06)]
    convert_element_type x15 -> x0, other arithmetic: 3.24 us -> none  [the longest x1 1.8 us: on_device(): image_low = image_unit.astype(jnp.bfloat16)]
  transfers between devices with their start and end apart: 25 -> 0, of which waited for: 15 -> 0; matrix products, arithmetic and copies ran while one was open for 14% -> 0% of each run, Pallas kernels for 0% -> 0%
where the time goes in v1:
time: 79.6 us; the launch traced here: 79.1 us
  Pallas kernels  73.1 us (92%)
  local copies, waits for them, and re-layouts  4.06 us (5%)
  between operations  1.94 us (2%)
    pallas_call x1, Pallas kernels, on_device(): pl.pallas_call(kernel, out_shape=(jax.ShapeDtypeStruct((B, width), jnp.fl...  73.1 us
    unnamed x7, local copies, waits for them, and re-layouts  4.06 us

profile of v1, /device:TPU:1, one launch (start us, length us, event | category | flops | bytes accessed | tf_op | source)
XLA Modules:
  0.0 79.1 jit_solution(14060127094638609073)
XLA Ops:
  1.9 0.0 copy-start
  1.9 1.0 %copy-done = bf16[128,1152]{1,0:T(8,128)(2,1)S(1)} copy-done((bf16[128,1152]{1,0:T(8,128)(2,1)S(1)}, bf16[128,1152]{1,0:T(8,128)(2,1)}, u32[]{:S(2)}) %copy-start) | copy-done | bytes 294936
  2.9 0.0 copy-start.1
  2.9 1.0 %copy-done.1 = bf16[128,1152]{1,0:T(8,128)(2,1)S(1)} copy-done((bf16[128,1152]{1,0:T(8,128)(2,1)S(1)}, bf16[128,1152]{1,0:T(8,128)(2,1)}, u32[]{:S(2)}) %copy-start.1) | copy-done | bytes 294936
  3.8 73.1 %window.1 = (f32[128,1152]{1,0:T(8,128)S(1)}, f32[128,1152]{1,0:T(8,128)S(1)}, f32[1,128]{1,0:T(1,128)S(1)}) custom-call(bf16[128,1152]{1,0:T(8,128)(2,1)S(1)} %copy-done, bf16[128,1152]{1,0:T(8,128)(2,1)S(1)} %copy-done.1, f32[1]{0:T(128)S(6)} %copy.10.log_scale, f32[1]{0:T(128)S(6)} %copy.11.bias), custom_call_target="tpu_custom_call" | custom-call | tf_op jit(solution)/shard_map/window/pallas_call | solution.py:347
  77.0 0.8 %copy.12 = f32[128,1152]{1,0:T(8,128)} copy(f32[128,1152]{1,0:T(8,128)S(1)} %get-tuple-element.12) | data formatting | bytes 1179648
  77.8 0.8 %copy.13 = f32[128,1152]{1,0:T(8,128)} copy(f32[128,1152]{1,0:T(8,128)S(1)} %get-tuple-element.13) | data formatting | bytes 1179648
  78.6 0.5 copy.14
Async XLA Ops:
  1.9 1.0 %copy-start = (bf16[128,1152]{1,0:T(8,128)(2,1)S(1)}, bf16[128,1152]{1,0:T(8,128)(2,1)}, u32[]{:S(2)}) copy-start(bf16[128,1152]{1,0:T(8,128)(2,1)} %images.1) | copy-start | bytes 884740
  2.9 1.0 %copy-start.1 = (bf16[128,1152]{1,0:T(8,128)(2,1)S(1)}, bf16[128,1152]{1,0:T(8,128)(2,1)}, u32[]{:S(2)}) copy-start(bf16[128,1152]{1,0:T(8,128)(2,1)} %texts.1) | copy-start | bytes 884740

commit v2 on v1

--- a/solution.py
+++ b/solution.py
@@ -11,8 +11,8 @@
 MESH = pl.DeviceIdType.MESH
 
 OWN, XM, XP, Y, YXM, YXP, X2, YX2 = range(8)
-T0B, T0A, T1A, T2A, T3A, T1B, T2B, T3B, RELAY = range(9)
-G1A, G1B, G2A, G2B, G3A, G3B, GR, GS = range(8)
+T0B, T0A, T1A, T2F, T3F, T1B, T2L, T3L, RELAY = range(9)
+G1A, G1B, G2F, G2L, G3F, G3L, GR, GS = range(8)
 
 
 def normalized(ref):
@@ -26,8 +26,8 @@
 
 
 def kernel(
-    images, texts, log_scale, bias, image_grad, text_grad, text_loss,
-    img, txt, pg, tgr, loss, sp, rxh, rx, sg, rg, sl, rl, ssem, rsem,
+    images_in, texts_in, log_scale, bias, image_grad, text_grad, text_loss,
+    images, texts, img, txt, pg, tgr, loss, sp, rxh, rx, sg, rg, sl, rl, isem, ssem, rsem,
 ):
     blk, member = lax.axis_index("blk"), lax.axis_index("member")
     n_blk, n_member = lax.axis_size("blk"), lax.axis_size("member")
@@ -40,6 +40,11 @@
     at_xp = (blk, (member + 2) % n_member)
     at_xm = (blk, (member + n_member - 2) % n_member)
     at_y = (blk, member + 1 - 2 * (member % 2))
+
+    image_load = pltpu.make_async_copy(images_in, images, isem.at[0])
+    text_load = pltpu.make_async_copy(texts_in, texts, isem.at[1])
+    image_load.start()
+    text_load.start()
 
     barrier = pltpu.get_barrier_semaphore()
     partners = (at_core, at_pair, at_zp, at_zm, at_xp, at_xm, at_y)
@@ -83,10 +88,10 @@
     f_z2 = copies(txt, T0A * B, txt, RELAY * B, B, at_zp, 2)
     f_c1a = copies(txt, T0A * B, txt, T1A * B, B, at_core)
     f_c1b = copies(txt, T0B * B, txt, T1B * B, B, at_core, 2, (txt, RELAY * B))
-    f_p2a = copies(txt, T0A * B, txt, T2A * B, B, at_pair, 2)
-    f_p2b = copies(txt, T0B * B, txt, T2B * B, B, at_pair, 2, (txt, RELAY * B))
-    f_c3a = copies(txt, T2A * B, txt, T3A * B, B, at_core)
-    f_c3b = copies(txt, T2B * B, txt, T3B * B, B, at_core)
+    f_p2f = copies(txt, T0B * B, txt, T2F * B, B, at_pair, 2, (txt, T0A * B))
+    f_p2l = copies(txt, T0A * B, txt, T2L * B, B, at_pair, 2, (txt, RELAY * B))
+    f_c3f = copies(txt, T2F * B, txt, T3F * B, B, at_core)
+    f_c3l = copies(txt, T2L * B, txt, T3L * B, B, at_core, 2)
     b_7t = copies(sp, YX2 * B, rxh, 0, HALF, at_xm)
     b_7b = copies(sp, YX2 * B + HALF, rxh, HALF, HALF, at_xp)
     b_6t = copies(sp, X2 * B, rxh, 2 * HALF, HALF, at_xm)
@@ -96,11 +101,11 @@
     b_1 = copies(sp, XM * B, rx, 2 * B, B, at_xm, 2)
     b_2 = copies(sp, XP * B, rx, 3 * B, B, at_xp, 2)
     b_3 = copies(sp, Y * B, rx, 4 * B, B, at_y, 2)
-    b_c3a = copies(sg, G3A * B, rg, G3A * B, B, at_core)
-    b_c3b = copies(sg, G3B * B, rg, G3B * B, B, at_core)
+    b_c3l = copies(sg, G3L * B, rg, G3L * B, B, at_core)
+    b_c3f = copies(sg, G3F * B, rg, G3F * B, B, at_core)
     b_c1 = copies(sg, G1A * B, rg, G1A * B, 2 * B, at_core)
-    b_p2b = copies(sg, G2B * B, rg, G2B * B, B, at_pair, 2)
-    b_p2a = copies(sg, G2A * B, rg, G2A * B, B, at_pair, 2)
+    b_p2l = copies(sg, G2L * B, rg, G2L * B, B, at_pair, 2)
+    b_p2f = copies(sg, G2F * B, rg, G2F * B, B, at_pair, 2)
     b_zr = copies(sg, GR * B, rg, GR * B, B, at_zm, 2)
     b_zs = copies(sg, GS * B, rg, GS * B, B, at_zm, 2)
     l_c = copies(sl, 0, rl, 0, 8, at_core)
@@ -125,8 +130,10 @@
     temper = jnp.exp(jnp.full((1, B), log_scale[0], jnp.float32))
     offset = bias[0]
 
+    image_load.wait()
     unit, _ = normalized(images)
     img[pl.ds(OWN * B, B), :] = unit.astype(jnp.bfloat16)
+    text_load.wait()
     unit, _ = normalized(texts)
     txt[pl.ds(T0B * B, B), :] = unit.astype(jnp.bfloat16)
 
@@ -137,10 +144,6 @@
     @pl.when(core == 0)
     def _():
         start_choice(f_c1b, 0)
-
-    @pl.when(y_lo == 0)
-    def _():
-        start_choice(f_p2b, 0)
 
     pg[...] = jnp.zeros_like(pg)
     tgr[...] = jnp.zeros_like(tgr)
@@ -190,15 +193,37 @@
 
         lax.fori_loop(0, slots // 2, body, 0)
 
-    landed(f_y)
-    start(f_yxp, f_yxm)
+    landed(f_y[:1])
+    start(f_yxp[:1])
+    landed(f_y[1:])
+    start(f_yxm[1:], f_yxm[:1], f_yxp[1:])
+
+    @pl.when(y_lo == 0)
+    def _():
+        start_choice(f_p2f, 0)
+
+    landed(f_z1[:1])
+    start(f_z2[:1])
+
+    @pl.when(y_lo == 1)
+    def _():
+        start_choice(f_p2f[:1], 1)
+
+    landed(f_z1[1:])
+    start(f_z2[1:])
+
+    @pl.when(y_lo == 1)
+    def _():
+        start_choice(f_p2f[1:], 1)
+
     landed(f_xp, f_xm)
-    start(f_x2t, f_x2b)
-    landed(f_z1)
-    start(f_z2, f_p2a, f_c1a)
+    start(f_x2t, f_x2b, f_c1a)
     tiles(OWN, 4, T0B, 2, diagonal=True)
-    landed(f_p2a)
-    start(f_c3a)
+
+    @pl.when(y_lo == 0)
+    def _():
+        start_choice(f_p2l, 0)
+
     landed(f_z2)
 
     @pl.when(core == 1)
@@ -207,83 +232,104 @@
 
     @pl.when(y_lo == 1)
     def _():
-        start_choice(f_p2b, 1)
-
-    landed(f_c1a, f_c3a, f_c1b)
-    landed(f_yxp, f_yxm)
-    start(f_yx2t, f_yx2b)
+        start_choice(f_p2l, 1)
+
+    landed(f_p2f)
+    start(f_c3f)
+    landed(f_yxp[:1])
+    start(f_yx2t)
+    landed(f_yxm[1:])
+    start(f_yx2b)
+    landed(f_c1a, f_c3f, f_c1b)
     tiles(OWN, 4, T1A, 4)
+    landed(f_yxp[1:], f_yxm[:1])
     tiles(YXM, 2, T0B, 6)
-    landed(f_p2b)
-    start(f_c3b)
-    landed(f_c3b, f_x2t, f_x2b, f_yx2t, f_yx2b)
-    tiles(X2, 2, T0B, 8)
-
-    def stage(slot):
-        sp[pl.ds(slot * B, B), :] = pg[pl.ds(slot * B, B), :].astype(jnp.bfloat16)
-
-    stage(YX2)
+    landed(f_p2l[:1])
+    start(f_c3l[:1])
+    landed(f_p2l[1:])
+    start(f_c3l[1:])
+    landed(f_x2t, f_x2b, f_yx2t, f_yx2b)
+    tiles(X2, 2, T0B, 6)
+    landed(f_c3l)
+    tiles(X2, 2, T2L, 2)
+
+    def stage(row, rows):
+        sp[pl.ds(row, rows), :] = pg[pl.ds(row, rows), :].astype(jnp.bfloat16)
+
+    def stage_sum(row, half):
+        total = pg[pl.ds(row, HALF), :] + rxh[pl.ds(half * HALF, HALF), :].astype(jnp.float32)
+        sp[pl.ds(row, HALF), :] = total.astype(jnp.bfloat16)
+
+    def text_sum(slot, k=0, rows=B):
+        return tgr[pl.ds(slot * B + k * HALF, rows), :]
+
+    def put(slot, value, k=0):
+        sg[pl.ds(slot * B + k * HALF, value.shape[0]), :] = value.astype(jnp.bfloat16)
+
+    def got(slot, k=0, rows=B):
+        return rg[pl.ds(slot * B + k * HALF, rows), :].astype(jnp.float32)
+
+    stage(YX2 * B, B)
     start(b_7t, b_7b)
-    stage(X2)
+    stage(X2 * B, B)
     start(b_6t, b_6b)
-    tiles(OWN, 6, T2B, 2)
-
-    def text_sum(slot):
-        return tgr[pl.ds(slot * B, B), :]
-
-    def put(slot, value):
-        sg[pl.ds(slot * B, B), :] = value.astype(jnp.bfloat16)
-
-    def got(slot):
-        return rg[pl.ds(slot * B, B), :].astype(jnp.float32)
-
-    put(G3B, text_sum(T3B))
-    start(b_c3b)
-    put(G3A, text_sum(T3A))
-    start(b_c3a)
+    tiles(OWN, 6, T2L, 2)
+    put(G3L, text_sum(T3L))
+    start(b_c3l)
+    stage(YXM * B + HALF, HALF)
+    start(b_4[1:])
+    stage(YXP * B, HALF)
+    start(b_5[:1])
+    put(G3F, text_sum(T3F))
+    start(b_c3f)
     sl[pl.ds(0, 8), :] = loss[...]
     start(l_c)
 
-    def pass_on(slot, top, half):
-        add = HALF * half
-        mine = pg[pl.ds(slot * B + (0 if top else HALF), HALF), :]
-        total = mine + rxh[pl.ds(add, HALF), :].astype(jnp.float32)
-        rest = slot * B + (HALF if top else 0)
-        sp[pl.ds(rest, HALF), :] = pg[pl.ds(rest, HALF), :].astype(jnp.bfloat16)
-        sp[pl.ds(slot * B + (0 if top else HALF), HALF), :] = total.astype(jnp.bfloat16)
-
-    landed(b_7t, b_7b)
-    pass_on(YXM, True, 0)
-    start(b_4)
-    pass_on(YXP, False, 1)
-    start(b_5)
-
-    landed(b_c3b)
-    put(G2B, text_sum(T2B) + got(G3B))
-    start(b_p2b)
-    landed(b_c3a)
-    put(G2A, text_sum(T2A) + got(G3A))
-    start(b_p2a)
+    for k in range(2):
+        if k == 0:
+            landed(b_c3l)
+        put(G2L, text_sum(T2L, k, HALF) + got(G3L, k, HALF), k)
+        start(b_p2l[k : k + 1])
+
+    landed(b_7t)
+    stage_sum(YXM * B, 0)
+    start(b_4[:1])
+    landed(b_7b)
+    stage_sum(YXP * B + HALF, 1)
+    start(b_5[1:])
+
     put(G1A, text_sum(T1A))
     put(G1B, text_sum(T1B))
     start(b_c1)
+    landed(b_c3f)
+    put(G2F, text_sum(T2F) + got(G3F))
     landed(l_c)
-    loss_2a = loss[pl.ds(T2A, 1), :] + rl[pl.ds(T3A, 1), :]
-    loss_2b = loss[pl.ds(T2B, 1), :] + rl[pl.ds(T3B, 1), :]
-    sl[pl.ds(8, 8), :] = jnp.concatenate([loss_2a, loss_2b] * 4, axis=0)
+    loss_2f = loss[pl.ds(T2F, 1), :] + rl[pl.ds(T3F, 1), :]
+    loss_2l = loss[pl.ds(T2L, 1), :] + rl[pl.ds(T3L, 1), :]
+    sl[pl.ds(8, 8), :] = jnp.concatenate([loss_2f, loss_2l] * 4, axis=0)
     start(l_p)
 
-    landed(b_6t, b_6b)
-    pass_on(XM, True, 2)
-    start(b_1)
-    pass_on(XP, False, 3)
-    start(b_2)
+    stage(XM * B + HALF, HALF)
+    start(b_1[1:])
+    stage(XP * B, HALF)
+    start(b_2[:1])
+    landed(b_6t)
+    stage_sum(XM * B, 2)
+    start(b_1[:1])
+    landed(b_6b)
+    stage_sum(XP * B + HALF, 3)
+    start(b_2[1:])
 
     odd = core.astype(jnp.float32)
     high = y_lo.astype(jnp.float32)
-    landed(b_c1, b_p2b)
-    put(GR, got(G1B) * odd + got(G2B) * high)
-    start(b_zr)
+    for c in b_p2l:
+        c.wait_send()
+    start(b_p2f)
+    landed(b_c1)
+    for k in range(2):
+        landed(b_p2l[k : k + 1])
+        put(GR, got(G1B, k, HALF) * odd + got(G2L, k, HALF) * high, k)
+        start(b_zr[k : k + 1])
     landed(l_p)
     sl[pl.ds(16, 8), :] = jnp.broadcast_to(
         rl[pl.ds(T1B, 1), :] * odd + rl[pl.ds(9, 1), :] * high, (8, B)
@@ -291,20 +337,28 @@
     start(l_zr)
 
     landed(b_4, b_5)
-    sp[pl.ds(Y * B, B), :] = (
-        pg[pl.ds(Y * B, B), :]
-        + rx[pl.ds(0 * B, B), :].astype(jnp.float32)
-        + rx[pl.ds(1 * B, B), :].astype(jnp.float32)
-    ).astype(jnp.bfloat16)
-    start(b_3)
-
-    landed(b_p2a)
-    landed(b_zr)
-    put(GS, text_sum(T0A) + got(G1A) + got(G2A) + got(GR))
-    start(b_zs)
+    for k in range(2):
+        total = (
+            pg[pl.ds(Y * B + k * HALF, HALF), :]
+            + rx[pl.ds(0 * B + k * HALF, HALF), :].astype(jnp.float32)
+            + rx[pl.ds(1 * B + k * HALF, HALF), :].astype(jnp.float32)
+        )
+        sp[pl.ds(Y * B + k * HALF, HALF), :] = total.astype(jnp.bfloat16)
+        start(b_3[k : k + 1])
+
+    for k in range(2):
+        landed(b_p2f[k : k + 1], b_zr[k : k + 1])
+        from_pair = got(G2F, k, HALF) * high + got(G2L, k, HALF) * (1.0 - high)
+        put(GS, text_sum(T0A, k, HALF) + got(G1A, k, HALF) + from_pair + got(GR, k, HALF), k)
+        start(b_zs[k : k + 1])
     landed(l_zr)
     sl[pl.ds(24, 8), :] = jnp.broadcast_to(
-        loss[pl.ds(T0A, 1), :] + rl[pl.ds(T1A, 1), :] + rl[pl.ds(8, 1), :] + rl[pl.ds(16, 1), :], (8, B)
+        loss[pl.ds(T0A, 1), :]
+        + rl[pl.ds(T1A, 1), :]
+        + rl[pl.ds(8, 1), :] * high
+        + rl[pl.ds(9, 1), :] * (1.0 - high)
+        + rl[pl.ds(16, 1), :],
+        (8, B),
     )
     start(l_zs)
 
@@ -322,18 +376,19 @@
 
     landed(b_zs, l_zs)
     own_sum = (
-        text_sum(T0B) + got(G1B) * (1.0 - odd) + got(G2B) * (1.0 - high) + got(GS)
+        text_sum(T0B) + got(G1B) * (1.0 - odd) + got(G2F) * (1.0 - high) + got(GS)
     )
     unit, inverse = normalized(texts)
     text_grad[...] = chain_back(unit, inverse, wide_temper * own_sum)
     text_loss[...] = (
         loss[pl.ds(T0B, 1), :]
         + rl[pl.ds(T1B, 1), :] * (1.0 - odd)
-        + rl[pl.ds(9, 1), :] * (1.0 - high)
+        + rl[pl.ds(8, 1), :] * (1.0 - high)
         + rl[pl.ds(24, 1), :]
     ) * (1.0 / STEPS)
     for c in sent:
-        c.wait_send()
+        if all(c is not done for done in b_p2l):
+            c.wait_send()
 
 
 SEMS = 80
@@ -341,6 +396,8 @@
 
 def on_device(images, texts, log_scale, bias):
     width = images.shape[1]
+    images = pltpu.with_memory_space_constraint(images, pltpu.HBM)
+    texts = pltpu.with_memory_space_constraint(texts, pltpu.HBM)
     rows = lambda n, dtype: pltpu.VMEM((n, width), dtype)
     vmem = pl.BlockSpec(memory_space=pltpu.VMEM)
     smem = pl.BlockSpec(memory_space=pltpu.SMEM)
@@ -351,9 +408,11 @@
             jax.ShapeDtypeStruct((B, width), jnp.float32),
             jax.ShapeDtypeStruct((1, B), jnp.float32),
         ),
-        in_specs=[vmem, vmem, smem, smem],
+        in_specs=[pl.BlockSpec(memory_space=pltpu.HBM)] * 2 + [smem, smem],
         out_specs=(vmem, vmem, vmem),
         scratch_shapes=[
+            rows(B, jnp.bfloat16),
+            rows(B, jnp.bfloat16),
             rows(8 * B, jnp.bfloat16),
             rows(9 * B, jnp.bfloat16),
             rows(8 * B, jnp.float32),
@@ -366,6 +425,7 @@
             rows(8 * B, jnp.bfloat16),
             pltpu.VMEM((32, B), jnp.float32),
             pltpu.VMEM((32, B), jnp.float32),
+            pltpu.SemaphoreType.DMA((2,)),
             pltpu.SemaphoreType.DMA((SEMS,)),
             pltpu.SemaphoreType.DMA((SEMS,)),
         ],

time: 79.6 us -> 72.7 us (0.913)
  Pallas kernels: 73.1 us -> 68.5 us
  local copies, waits for them, and re-layouts: 4.06 us -> 2.14 us
    pallas_call x1, Pallas kernels: 73.1 us -> 68.5 us  [on_device(): pl.pallas_call(kernel, out_shape=(jax.ShapeDtypeStruct((B, width), jnp.fl...]
    unnamed x7 -> x3, local copies, waits for them, and re-layouts: 4.06 us -> 2.14 us
where the time goes in v2:
time: 72.7 us; the launch traced here: 72.6 us
  Pallas kernels  68.5 us (94%)
  local copies, waits for them, and re-layouts  2.14 us (3%)
  between operations  1.93 us (3%)
    pallas_call x1, Pallas kernels, on_device(): pl.pallas_call(kernel, out_shape=(jax.ShapeDtypeStruct((B, width), jnp.fl...  68.5 us
    unnamed x3, local copies, waits for them, and re-layouts  2.14 us

profile of v2, /device:TPU:1, one launch (start us, length us, event | category | flops | bytes accessed | tf_op | source)
XLA Modules:
  0.0 72.6 jit_solution(16909433036713226370)
XLA Ops:
  1.9 68.5 %window.1 = (f32[128,1152]{1,0:T(8,128)S(1)}, f32[128,1152]{1,0:T(8,128)S(1)}, f32[1,128]{1,0:T(1,128)S(1)}) custom-call(bf16[128,1152]{1,0:T(8,128)(2,1)} %images_in.1, bf16[128,1152]{1,0:T(8,128)(2,1)} %texts_in.1, f32[1]{0:T(128)S(6)} %copy.10.log_scale, f32[1]{0:T(128)S(6)} %copy.11.bias), custom_call_target="tpu_custom_call" | custom-call | tf_op jit(solution)/shard_map/window/pallas_call | solution.py:404
  70.4 0.8 %copy.12 = f32[128,1152]{1,0:T(8,128)} copy(f32[128,1152]{1,0:T(8,128)S(1)} %get-tuple-element.12) | data formatting | bytes 1179648
  71.3 0.8 %copy.13 = f32[128,1152]{1,0:T(8,128)} copy(f32[128,1152]{1,0:T(8,128)S(1)} %get-tuple-element.13) | data formatting | bytes 1179648
  72.1 0.5 copy.14

commit v3 on v2

--- a/solution.py
+++ b/solution.py
@@ -11,8 +11,8 @@
 MESH = pl.DeviceIdType.MESH
 
 OWN, XM, XP, Y, YXM, YXP, X2, YX2 = range(8)
-T0B, T0A, T1A, T2F, T3F, T1B, T2L, T3L, RELAY = range(9)
-G1A, G1B, G2F, G2L, G3F, G3L, GR, GS = range(8)
+T0B, T0A, T1A, T1B, T2F, T3F, T2L, T3L, RELAY = range(9)
+G1A, G1B, G2F, G2L, G3F, G3L, GZ, GR, GS = range(9)
 
 
 def normalized(ref):
@@ -52,7 +52,6 @@
         pl.semaphore_signal(barrier, inc=1, device_id=device, device_id_type=MESH)
 
     used = [0]
-    sent = []
 
     def copies(src, src_row, dst, dst_row, rows, device, pieces=1, other=None):
         out = []
@@ -71,7 +70,6 @@
                 )
                 for a, r in [(src, src_row)] + ([other] if other else [])
             ]
-            sent.append(made[0])
             out.append(made if other else made[0])
         return out
 
@@ -85,11 +83,12 @@
     f_yx2t = copies(img, YXM * B, img, YX2 * B, HALF, at_xp)
     f_yx2b = copies(img, YXP * B + HALF, img, YX2 * B + HALF, HALF, at_xm)
     f_z1 = copies(txt, T0B * B, txt, T0A * B, B, at_zp, 2)
+    f_c1a = copies(txt, T0A * B, txt, T1A * B, B, at_core)
     f_z2 = copies(txt, T0A * B, txt, RELAY * B, B, at_zp, 2)
-    f_c1a = copies(txt, T0A * B, txt, T1A * B, B, at_core)
-    f_c1b = copies(txt, T0B * B, txt, T1B * B, B, at_core, 2, (txt, RELAY * B))
+    f_c1b = copies(txt, T0B * B, txt, T1B * B, B, at_core, 1, (txt, RELAY * B))
     f_p2f = copies(txt, T0B * B, txt, T2F * B, B, at_pair, 2, (txt, T0A * B))
-    f_p2l = copies(txt, T0A * B, txt, T2L * B, B, at_pair, 2, (txt, RELAY * B))
+    f_p2l = copies(txt, T0A * B, txt, T2L * B, B, at_pair, 2)
+    f_zf = copies(txt, T2F * B, txt, T2L * B, B, at_zp, 2)
     f_c3f = copies(txt, T2F * B, txt, T3F * B, B, at_core)
     f_c3l = copies(txt, T2L * B, txt, T3L * B, B, at_core, 2)
     b_7t = copies(sp, YX2 * B, rxh, 0, HALF, at_xm)
@@ -101,17 +100,19 @@
     b_1 = copies(sp, XM * B, rx, 2 * B, B, at_xm, 2)
     b_2 = copies(sp, XP * B, rx, 3 * B, B, at_xp, 2)
     b_3 = copies(sp, Y * B, rx, 4 * B, B, at_y, 2)
-    b_c3l = copies(sg, G3L * B, rg, G3L * B, B, at_core)
+    b_c3l = copies(sg, G3L * B, rg, G3L * B, B, at_core, 2)
     b_c3f = copies(sg, G3F * B, rg, G3F * B, B, at_core)
     b_c1 = copies(sg, G1A * B, rg, G1A * B, 2 * B, at_core)
+    b_zf = copies(sg, G2L * B, rg, GZ * B, B, at_zm, 2)
     b_p2l = copies(sg, G2L * B, rg, G2L * B, B, at_pair, 2)
     b_p2f = copies(sg, G2F * B, rg, G2F * B, B, at_pair, 2)
-    b_zr = copies(sg, GR * B, rg, GR * B, B, at_zm, 2)
+    b_zr = copies(rg, G1B * B, rg, GR * B, B, at_zm)
     b_zs = copies(sg, GS * B, rg, GS * B, B, at_zm, 2)
     l_c = copies(sl, 0, rl, 0, 8, at_core)
-    l_p = copies(sl, 8, rl, 8, 8, at_pair)
-    l_zr = copies(sl, 16, rl, 16, 8, at_zm)
-    l_zs = copies(sl, 24, rl, 24, 8, at_zm)
+    l_zf = copies(sl, 8, rl, 8, 8, at_zm)
+    l_p = copies(sl, 16, rl, 16, 8, at_pair)
+    l_zr = copies(rl, 0, rl, 24, 8, at_zm)
+    l_zs = copies(sl, 24, rl, 32, 8, at_zm)
 
     def start(*lists):
         for group in lists:
@@ -123,6 +124,11 @@
             for c in group:
                 (c[0] if isinstance(c, list) else c).wait_recv()
 
+    def left(*lists):
+        for group in lists:
+            for c in group:
+                (c[0] if isinstance(c, list) else c).wait_send()
+
     def start_choice(group, which):
         for c in group:
             c[which].start()
@@ -133,13 +139,14 @@
     image_load.wait()
     unit, _ = normalized(images)
     img[pl.ds(OWN * B, B), :] = unit.astype(jnp.bfloat16)
+
+    pl.semaphore_wait(barrier, len(partners))
+
+    start(f_y, f_xp, f_xm)
     text_load.wait()
     unit, _ = normalized(texts)
     txt[pl.ds(T0B * B, B), :] = unit.astype(jnp.bfloat16)
-
-    pl.semaphore_wait(barrier, len(partners))
-
-    start(f_y, f_xp, f_xm, f_z1)
+    start(f_z1)
 
     @pl.when(core == 0)
     def _():
@@ -185,16 +192,14 @@
             low, i, (((0,), (0,)), ((), ())), preferred_element_type=jnp.float32
         )
 
-    def tiles(first_slot, slots, first, blocks, diagonal=False):
-        def body(k, carry):
-            row = pl.multiple_of((first_slot + 2 * k) * B, 2 * B)
-            tile(row, 2 * B, first, blocks, diagonal)
-            return carry
-
-        lax.fori_loop(0, slots // 2, body, 0)
-
     landed(f_y[:1])
     start(f_yxp[:1])
+    landed(f_z1[:1])
+
+    @pl.when(core == 1)
+    def _():
+        start(f_z2[:1])
+
     landed(f_y[1:])
     start(f_yxm[1:], f_yxm[:1], f_yxp[1:])
 
@@ -202,56 +207,76 @@
     def _():
         start_choice(f_p2f, 0)
 
-    landed(f_z1[:1])
-    start(f_z2[:1])
-
     @pl.when(y_lo == 1)
     def _():
         start_choice(f_p2f[:1], 1)
 
     landed(f_z1[1:])
-    start(f_z2[1:])
+
+    @pl.when(core == 1)
+    def _():
+        start(f_z2[1:])
 
     @pl.when(y_lo == 1)
     def _():
         start_choice(f_p2f[1:], 1)
 
+    start(f_c1a)
     landed(f_xp, f_xm)
-    start(f_x2t, f_x2b, f_c1a)
-    tiles(OWN, 4, T0B, 2, diagonal=True)
-
-    @pl.when(y_lo == 0)
-    def _():
-        start_choice(f_p2l, 0)
-
-    landed(f_z2)
-
-    @pl.when(core == 1)
-    def _():
-        start_choice(f_c1b, 1)
-
-    @pl.when(y_lo == 1)
-    def _():
-        start_choice(f_p2l, 1)
-
-    landed(f_p2f)
-    start(f_c3f)
+    start(f_x2t, f_x2b)
+    tile(OWN * B, 4 * B, T0B, 2, diagonal=True)
+
+    @pl.when(y_lo == 0)
+    def _():
+        start(f_p2l)
+
     landed(f_yxp[:1])
     start(f_yx2t)
     landed(f_yxm[1:])
     start(f_yx2b)
-    landed(f_c1a, f_c3f, f_c1b)
-    tiles(OWN, 4, T1A, 4)
+
+    @pl.when(y_lo == 0)
+    def _():
+        landed(f_p2f[:1])
+        start(f_zf[:1])
+
+    @pl.when(core == 1)
+    def _():
+        landed(f_z2)
+        start_choice(f_c1b, 1)
+
+    landed(f_c1a, f_c1b)
+    tile(OWN * B, 4 * B, T1A, 2)
+
+    @pl.when(y_lo == 0)
+    def _():
+        landed(f_p2f[1:])
+        start(f_zf[1:])
+
+    @pl.when(y_lo == 1)
+    def _():
+        landed(f_p2f)
+
+    start(f_c3f)
+    landed(f_c3f)
+    tile(OWN * B, 4 * B, T2F, 2)
     landed(f_yxp[1:], f_yxm[:1])
-    tiles(YXM, 2, T0B, 6)
-    landed(f_p2l[:1])
-    start(f_c3l[:1])
-    landed(f_p2l[1:])
-    start(f_c3l[1:])
+    tile(YXM * B, 2 * B, T0B, 6)
+    for k in range(2):
+
+        @pl.when(y_lo == 0)
+        def _():
+            landed(f_zf[k : k + 1])
+
+        @pl.when(y_lo == 1)
+        def _():
+            landed(f_p2l[k : k + 1])
+
+        start(f_c3l[k : k + 1])
+    landed(f_c3l)
+    tile(YXM * B, 2 * B, T2L, 2)
     landed(f_x2t, f_x2b, f_yx2t, f_yx2b)
-    tiles(X2, 2, T0B, 6)
-    landed(f_c3l)
-    tiles(X2, 2, T2L, 2)
+    tile(X2 * B, 2 * B, T0B, 8)
 
     def stage(row, rows):
         sp[pl.ds(row, rows), :] = pg[pl.ds(row, rows), :].astype(jnp.bfloat16)
@@ -271,25 +296,23 @@
 
     stage(YX2 * B, B)
     start(b_7t, b_7b)
-    stage(X2 * B, B)
-    start(b_6t, b_6b)
-    tiles(OWN, 6, T2L, 2)
-    put(G3L, text_sum(T3L))
-    start(b_c3l)
     stage(YXM * B + HALF, HALF)
     start(b_4[1:])
     stage(YXP * B, HALF)
     start(b_5[:1])
     put(G3F, text_sum(T3F))
     start(b_c3f)
+    put(G1A, text_sum(T1A))
+    put(G1B, text_sum(T1B))
+    start(b_c1)
+    stage(X2 * B, B)
+    start(b_6t, b_6b)
+    tile(OWN * B, 4 * B, T2L, 2)
+    for k in range(2):
+        put(G3L, text_sum(T3L, k, HALF), k)
+        start(b_c3l[k : k + 1])
     sl[pl.ds(0, 8), :] = loss[...]
     start(l_c)
-
-    for k in range(2):
-        if k == 0:
-            landed(b_c3l)
-        put(G2L, text_sum(T2L, k, HALF) + got(G3L, k, HALF), k)
-        start(b_p2l[k : k + 1])
 
     landed(b_7t)
     stage_sum(YXM * B, 0)
@@ -298,16 +321,40 @@
     stage_sum(YXP * B + HALF, 1)
     start(b_5[1:])
 
-    put(G1A, text_sum(T1A))
-    put(G1B, text_sum(T1B))
-    start(b_c1)
-    landed(b_c3f)
-    put(G2F, text_sum(T2F) + got(G3F))
-    landed(l_c)
+    for k in range(2):
+        landed(b_c3l[k : k + 1])
+        put(G2L, text_sum(T2L, k, HALF) + got(G3L, k, HALF), k)
+
+        @pl.when(y_lo == 0)
+        def _():
+            start(b_zf[k : k + 1])
+
+        @pl.when(y_lo == 1)
+        def _():
+            start(b_p2l[k : k + 1])
+
+    landed(b_c3f, l_c)
     loss_2f = loss[pl.ds(T2F, 1), :] + rl[pl.ds(T3F, 1), :]
     loss_2l = loss[pl.ds(T2L, 1), :] + rl[pl.ds(T3L, 1), :]
-    sl[pl.ds(8, 8), :] = jnp.concatenate([loss_2f, loss_2l] * 4, axis=0)
-    start(l_p)
+
+    @pl.when(y_lo == 0)
+    def _():
+        sl[pl.ds(8, 8), :] = jnp.broadcast_to(loss_2l, (8, B))
+        start(l_zf)
+
+    landed(b_c1)
+
+    @pl.when(core == 1)
+    def _():
+        start(b_zr, l_zr)
+
+    @pl.when(y_lo == 1)
+    def _():
+        sl[pl.ds(16, 8), :] = jnp.concatenate([loss_2f, loss_2l] * 4, axis=0)
+        start(l_p)
+        put(G2F, text_sum(T2F) + got(G3F))
+        left(b_p2l)
+        start(b_p2f)
 
     stage(XM * B + HALF, HALF)
     start(b_1[1:])
@@ -320,21 +367,16 @@
     stage_sum(XP * B + HALF, 3)
     start(b_2[1:])
 
-    odd = core.astype(jnp.float32)
-    high = y_lo.astype(jnp.float32)
-    for c in b_p2l:
-        c.wait_send()
-    start(b_p2f)
-    landed(b_c1)
-    for k in range(2):
-        landed(b_p2l[k : k + 1])
-        put(GR, got(G1B, k, HALF) * odd + got(G2L, k, HALF) * high, k)
-        start(b_zr[k : k + 1])
-    landed(l_p)
-    sl[pl.ds(16, 8), :] = jnp.broadcast_to(
-        rl[pl.ds(T1B, 1), :] * odd + rl[pl.ds(9, 1), :] * high, (8, B)
-    )
-    start(l_zr)
+    @pl.when(y_lo == 0)
+    def _():
+        for k in range(2):
+            landed(b_zf[k : k + 1])
+            total = text_sum(T2F, k, HALF) + got(G3F, k, HALF) + got(GZ, k, HALF)
+            put(G2F, total, k)
+            start(b_p2f[k : k + 1])
+        landed(l_zf)
+        sl[pl.ds(16, 8), :] = jnp.broadcast_to(loss_2f + rl[pl.ds(8, 1), :], (8, B))
+        start(l_p)
 
     landed(b_4, b_5)
     for k in range(2):
@@ -346,21 +388,46 @@
         sp[pl.ds(Y * B + k * HALF, HALF), :] = total.astype(jnp.bfloat16)
         start(b_3[k : k + 1])
 
+    @pl.when(core == 1)
+    def _():
+        landed(b_zr, l_zr)
+        tgr[pl.ds(T0A * B, B), :] += got(GR)
+        loss[pl.ds(T0A, 1), :] += rl[pl.ds(24 + T1B, 1), :]
+
     for k in range(2):
-        landed(b_p2f[k : k + 1], b_zr[k : k + 1])
-        from_pair = got(G2F, k, HALF) * high + got(G2L, k, HALF) * (1.0 - high)
-        put(GS, text_sum(T0A, k, HALF) + got(G1A, k, HALF) + from_pair + got(GR, k, HALF), k)
+
+        @pl.when(y_lo == 0)
+        def _():
+            landed(b_p2l[k : k + 1])
+            put(GS, text_sum(T0A, k, HALF) + got(G1A, k, HALF) + got(G2L, k, HALF), k)
+
+        @pl.when(y_lo == 1)
+        def _():
+            landed(b_p2f[k : k + 1])
+            put(GS, text_sum(T0A, k, HALF) + got(G1A, k, HALF) + got(G2F, k, HALF), k)
+
         start(b_zs[k : k + 1])
-    landed(l_zr)
-    sl[pl.ds(24, 8), :] = jnp.broadcast_to(
-        loss[pl.ds(T0A, 1), :]
-        + rl[pl.ds(T1A, 1), :]
-        + rl[pl.ds(8, 1), :] * high
-        + rl[pl.ds(9, 1), :] * (1.0 - high)
-        + rl[pl.ds(16, 1), :],
-        (8, B),
-    )
+
+    landed(l_p)
+    loss_s = loss[pl.ds(T0A, 1), :] + rl[pl.ds(T1A, 1), :]
+
+    @pl.when(y_lo == 0)
+    def _():
+        sl[pl.ds(24, 8), :] = jnp.broadcast_to(loss_s + rl[pl.ds(17, 1), :], (8, B))
+        landed(b_p2f)
+        tgr[pl.ds(T0B * B, B), :] += got(G2F)
+        loss[pl.ds(T0B, 1), :] += rl[pl.ds(16, 1), :]
+
+    @pl.when(y_lo == 1)
+    def _():
+        sl[pl.ds(24, 8), :] = jnp.broadcast_to(loss_s + rl[pl.ds(16, 1), :], (8, B))
+
     start(l_zs)
+
+    @pl.when(core == 0)
+    def _():
+        tgr[pl.ds(T0B * B, B), :] += got(G1B)
+        loss[pl.ds(T0B, 1), :] += rl[pl.ds(T1B, 1), :]
 
     wide_temper = jnp.concatenate([temper] * (images.shape[1] // B), axis=1)
 
@@ -375,20 +442,22 @@
     image_grad[...] = chain_back(unit, inverse, wide_temper * image_sum)
 
     landed(b_zs, l_zs)
-    own_sum = (
-        text_sum(T0B) + got(G1B) * (1.0 - odd) + got(G2F) * (1.0 - high) + got(GS)
-    )
     unit, inverse = normalized(texts)
-    text_grad[...] = chain_back(unit, inverse, wide_temper * own_sum)
-    text_loss[...] = (
-        loss[pl.ds(T0B, 1), :]
-        + rl[pl.ds(T1B, 1), :] * (1.0 - odd)
-        + rl[pl.ds(8, 1), :] * (1.0 - high)
-        + rl[pl.ds(24, 1), :]
-    ) * (1.0 / STEPS)
-    for c in sent:
-        if all(c is not done for done in b_p2l):
-            c.wait_send()
+    text_grad[...] = chain_back(unit, inverse, wide_temper * (text_sum(T0B) + got(GS)))
+    text_loss[...] = (loss[pl.ds(T0B, 1), :] + rl[pl.ds(32, 1), :]) * (1.0 / STEPS)
+
+    left(f_xp, f_xm, f_y, f_x2t, f_x2b, f_yxp, f_yxm, f_yx2t, f_yx2b)
+    left(f_z1, f_c1a, f_c1b, f_p2f, f_c3f, f_c3l)
+    left(b_7t, b_7b, b_6t, b_6b, b_4, b_5, b_1, b_2, b_3)
+    left(b_c3l, b_c3f, b_c1, b_p2f, b_zs, l_c, l_p, l_zs)
+
+    @pl.when(core == 1)
+    def _():
+        left(f_z2, b_zr, l_zr)
+
+    @pl.when(y_lo == 0)
+    def _():
+        left(f_p2l, f_zf, b_zf, l_zf)
 
 
 SEMS = 80
@@ -421,10 +490,10 @@
             rows(8 * B, jnp.bfloat16),
             rows(4 * HALF, jnp.bfloat16),
             rows(5 * B, jnp.bfloat16),
-            rows(8 * B, jnp.bfloat16),
-            rows(8 * B, jnp.bfloat16),
+            rows(9 * B, jnp.bfloat16),
+            rows(9 * B, jnp.bfloat16),
             pltpu.VMEM((32, B), jnp.float32),
-            pltpu.VMEM((32, B), jnp.float32),
+            pltpu.VMEM((40, B), jnp.float32),
             pltpu.SemaphoreType.DMA((2,)),
             pltpu.SemaphoreType.DMA((SEMS,)),
             pltpu.SemaphoreType.DMA((SEMS,)),

time: 72.7 us -> 73.9 us (1.017)
  Pallas kernels: 68.5 us -> 69.7 us
    pallas_call x1, Pallas kernels: 68.5 us -> 69.7 us  [on_device(): pl.pallas_call(kernel, out_shape=(jax.ShapeDtypeStruct((B, width), jnp.fl...]
where the time goes in v3:
time: 73.9 us; the launch traced here: 73.8 us
  Pallas kernels  69.7 us (94%)
  local copies, waits for them, and re-layouts  2.14 us (3%)
  between operations  1.93 us (3%)
    pallas_call x1, Pallas kernels, on_device(): pl.pallas_call(kernel, out_shape=(jax.ShapeDtypeStruct((B, width), jnp.fl...  69.7 us
    unnamed x3, local copies, waits for them, and re-layouts  2.14 us

profile of v3, /device:TPU:1, one launch (start us, length us, event | category | flops | bytes accessed | tf_op | source)
XLA Modules:
  0.0 73.8 jit_solution(2381345492603306017)
XLA Ops:
  1.9 69.7 %window.1 = (f32[128,1152]{1,0:T(8,128)S(1)}, f32[128,1152]{1,0:T(8,128)S(1)}, f32[1,128]{1,0:T(1,128)S(1)}) custom-call(bf16[128,1152]{1,0:T(8,128)(2,1)} %images_in.1, bf16[128,1152]{1,0:T(8,128)(2,1)} %texts_in.1, f32[1]{0:T(128)S(6)} %copy.10.log_scale, f32[1]{0:T(128)S(6)} %copy.11.bias), custom_call_target="tpu_custom_call" | custom-call | tf_op jit(solution)/shard_map/window/pallas_call | solution.py:473
  71.6 0.8 %copy.12 = f32[128,1152]{1,0:T(8,128)} copy(f32[128,1152]{1,0:T(8,128)S(1)} %get-tuple-element.12) | data formatting | bytes 1179648
  72.5 0.8 %copy.13 = f32[128,1152]{1,0:T(8,128)} copy(f32[128,1152]{1,0:T(8,128)S(1)} %get-tuple-element.13) | data formatting | bytes 1179648
  73.3 0.5 copy.14

commit v4 on v2

--- a/solution.py
+++ b/solution.py
@@ -11,7 +11,7 @@
 MESH = pl.DeviceIdType.MESH
 
 OWN, XM, XP, Y, YXM, YXP, X2, YX2 = range(8)
-T0B, T0A, T1A, T2F, T3F, T1B, T2L, T3L, RELAY = range(9)
+T0B, T0A, T1A, T1B, T2F, T3F, T2L, T3L, RELAY = range(9)
 G1A, G1B, G2F, G2L, G3F, G3L, GR, GS = range(8)
 
 
@@ -33,6 +33,7 @@
     n_blk, n_member = lax.axis_size("blk"), lax.axis_size("member")
     core = blk % 2
     y_lo = (blk // 2) % 2
+    z = blk // 4
     at_core = (blk + 1 - 2 * core, member)
     at_pair = (blk + 2 - 4 * y_lo, member)
     at_zp = ((blk + 4) % n_blk, member)
@@ -47,12 +48,11 @@
     text_load.start()
 
     barrier = pltpu.get_barrier_semaphore()
-    partners = (at_core, at_pair, at_zp, at_zm, at_xp, at_xm, at_y)
+    partners = (at_core, at_pair, at_zm, at_xp, at_xm, at_y)
     for device in partners:
         pl.semaphore_signal(barrier, inc=1, device_id=device, device_id_type=MESH)
 
     used = [0]
-    sent = []
 
     def copies(src, src_row, dst, dst_row, rows, device, pieces=1, other=None):
         out = []
@@ -71,7 +71,6 @@
                 )
                 for a, r in [(src, src_row)] + ([other] if other else [])
             ]
-            sent.append(made[0])
             out.append(made if other else made[0])
         return out
 
@@ -85,11 +84,12 @@
     f_yx2t = copies(img, YXM * B, img, YX2 * B, HALF, at_xp)
     f_yx2b = copies(img, YXP * B + HALF, img, YX2 * B + HALF, HALF, at_xm)
     f_z1 = copies(txt, T0B * B, txt, T0A * B, B, at_zp, 2)
+    f_c1a = copies(txt, T0A * B, txt, T1A * B, B, at_core)
     f_z2 = copies(txt, T0A * B, txt, RELAY * B, B, at_zp, 2)
-    f_c1a = copies(txt, T0A * B, txt, T1A * B, B, at_core)
-    f_c1b = copies(txt, T0B * B, txt, T1B * B, B, at_core, 2, (txt, RELAY * B))
+    f_c1b = copies(txt, T0B * B, txt, T1B * B, B, at_core, 1, (txt, RELAY * B))
     f_p2f = copies(txt, T0B * B, txt, T2F * B, B, at_pair, 2, (txt, T0A * B))
-    f_p2l = copies(txt, T0A * B, txt, T2L * B, B, at_pair, 2, (txt, RELAY * B))
+    f_p2l = copies(txt, T0A * B, txt, T2L * B, B, at_pair, 2)
+    f_zf = copies(txt, T2F * B, txt, T2L * B, B, at_zp, 2)
     f_c3f = copies(txt, T2F * B, txt, T3F * B, B, at_core)
     f_c3l = copies(txt, T2L * B, txt, T3L * B, B, at_core, 2)
     b_7t = copies(sp, YX2 * B, rxh, 0, HALF, at_xm)
@@ -101,7 +101,7 @@
     b_1 = copies(sp, XM * B, rx, 2 * B, B, at_xm, 2)
     b_2 = copies(sp, XP * B, rx, 3 * B, B, at_xp, 2)
     b_3 = copies(sp, Y * B, rx, 4 * B, B, at_y, 2)
-    b_c3l = copies(sg, G3L * B, rg, G3L * B, B, at_core)
+    b_c3l = copies(sg, G3L * B, rg, G3L * B, B, at_core, 2)
     b_c3f = copies(sg, G3F * B, rg, G3F * B, B, at_core)
     b_c1 = copies(sg, G1A * B, rg, G1A * B, 2 * B, at_core)
     b_p2l = copies(sg, G2L * B, rg, G2L * B, B, at_pair, 2)
@@ -123,6 +123,11 @@
             for c in group:
                 (c[0] if isinstance(c, list) else c).wait_recv()
 
+    def left(*lists):
+        for group in lists:
+            for c in group:
+                (c[0] if isinstance(c, list) else c).wait_send()
+
     def start_choice(group, which):
         for c in group:
             c[which].start()
@@ -130,16 +135,17 @@
     temper = jnp.exp(jnp.full((1, B), log_scale[0], jnp.float32))
     offset = bias[0]
 
+    text_load.wait()
+    unit, _ = normalized(texts)
+    txt[pl.ds(T0B * B, B), :] = unit.astype(jnp.bfloat16)
+
+    pl.semaphore_wait(barrier, len(partners))
+
+    start(f_z1)
     image_load.wait()
     unit, _ = normalized(images)
     img[pl.ds(OWN * B, B), :] = unit.astype(jnp.bfloat16)
-    text_load.wait()
-    unit, _ = normalized(texts)
-    txt[pl.ds(T0B * B, B), :] = unit.astype(jnp.bfloat16)
-
-    pl.semaphore_wait(barrier, len(partners))
-
-    start(f_y, f_xp, f_xm, f_z1)
+    start(f_y, f_xp, f_xm)
 
     @pl.when(core == 0)
     def _():
@@ -185,73 +191,88 @@
             low, i, (((0,), (0,)), ((), ())), preferred_element_type=jnp.float32
         )
 
-    def tiles(first_slot, slots, first, blocks, diagonal=False):
-        def body(k, carry):
-            row = pl.multiple_of((first_slot + 2 * k) * B, 2 * B)
-            tile(row, 2 * B, first, blocks, diagonal)
-            return carry
-
-        lax.fori_loop(0, slots // 2, body, 0)
-
-    landed(f_y[:1])
-    start(f_yxp[:1])
-    landed(f_y[1:])
-    start(f_yxm[1:], f_yxm[:1], f_yxp[1:])
+    def from_z(k):
+        landed(f_z1[k : k + 1])
+
+        @pl.when(core == 1)
+        def _():
+            start(f_z2[k : k + 1])
+
+        @pl.when(y_lo == 1)
+        def _():
+            start_choice(f_p2f[k : k + 1], 1)
+
+    def from_y(k):
+        landed(f_y[k : k + 1])
+        if k == 0:
+            start(f_yxp[:1])
+        else:
+            start(f_yxm[1:], f_yxm[:1], f_yxp[1:])
+
+            @pl.when(y_lo == 0)
+            def _():
+                start_choice(f_p2f, 0)
+
+    def round_x():
+        landed(f_xp, f_xm)
+        start(f_x2t, f_x2b)
+
+    def round_yx():
+        landed(f_yxp[:1])
+        start(f_yx2t)
+        landed(f_yxm[1:])
+        start(f_yx2b)
+
+    @pl.when(z == 0)
+    def _():
+        from_y(0)
+        from_y(1)
+        round_x()
+        round_yx()
+        from_z(0)
+        from_z(1)
+
+    @pl.when(z > 0)
+    def _():
+        from_z(0)
+        from_y(0)
+        from_z(1)
+        from_y(1)
+        round_x()
+
+    start(f_c1a)
+    tile(OWN * B, 4 * B, T0B, 2, diagonal=True)
+
+    @pl.when(z > 0)
+    def _():
+        round_yx()
 
     @pl.when(y_lo == 0)
     def _():
-        start_choice(f_p2f, 0)
-
-    landed(f_z1[:1])
-    start(f_z2[:1])
+        start(f_p2l)
+        landed(f_p2f[:1])
+        start(f_zf[:1])
+        landed(f_p2f[1:])
+        start(f_zf[1:])
+
+    @pl.when(core == 1)
+    def _():
+        landed(f_z2)
+        start_choice(f_c1b, 1)
+
+    landed(f_c1a, f_c1b)
+    tile(OWN * B, 4 * B, T1A, 2)
 
     @pl.when(y_lo == 1)
     def _():
-        start_choice(f_p2f[:1], 1)
-
-    landed(f_z1[1:])
-    start(f_z2[1:])
-
-    @pl.when(y_lo == 1)
-    def _():
-        start_choice(f_p2f[1:], 1)
-
-    landed(f_xp, f_xm)
-    start(f_x2t, f_x2b, f_c1a)
-    tiles(OWN, 4, T0B, 2, diagonal=True)
-
-    @pl.when(y_lo == 0)
-    def _():
-        start_choice(f_p2l, 0)
-
-    landed(f_z2)
-
-    @pl.when(core == 1)
-    def _():
-        start_choice(f_c1b, 1)
-
-    @pl.when(y_lo == 1)
-    def _():
-        start_choice(f_p2l, 1)
-
-    landed(f_p2f)
+        landed(f_p2f)
+
     start(f_c3f)
-    landed(f_yxp[:1])
-    start(f_yx2t)
-    landed(f_yxm[1:])
-    start(f_yx2b)
-    landed(f_c1a, f_c3f, f_c1b)
-    tiles(OWN, 4, T1A, 4)
-    landed(f_yxp[1:], f_yxm[:1])
-    tiles(YXM, 2, T0B, 6)
-    landed(f_p2l[:1])
-    start(f_c3l[:1])
-    landed(f_p2l[1:])
-    start(f_c3l[1:])
+    landed(f_yxp[1:], f_yxm[:1], f_c3f)
+    tile(OWN * B, 4 * B, T2F, 2)
+    tile(YXM * B, 2 * B, T0B, 6)
     landed(f_x2t, f_x2b, f_yx2t, f_yx2b)
-    tiles(X2, 2, T0B, 6)
-    landed(f_c3l)
-    tiles(X2, 2, T2L, 2)
+    tile(X2 * B, 2 * B, T0B, 6)
 
     def stage(row, rows):
         sp[pl.ds(row, rows), :] = pg[pl.ds(row, rows), :].astype(jnp.bfloat16)
@@ -269,27 +290,39 @@
     def got(slot, k=0, rows=B):
         return rg[pl.ds(slot * B + k * HALF, rows), :].astype(jnp.float32)
 
+    for k in range(2):
+
+        @pl.when(y_lo == 0)
+        def _():
+            landed(f_zf[k : k + 1])
+
+        @pl.when(y_lo == 1)
+        def _():
+            landed(f_p2l[k : k + 1])
+
+        start(f_c3l[k : k + 1])
+    put(G3F, text_sum(T3F))
+    start(b_c3f)
+    put(G1A, text_sum(T1A))
+    put(G1B, text_sum(T1B))
+    start(b_c1)
+    landed(f_c3l)
+    tile(X2 * B, 2 * B, T2L, 2)
     stage(YX2 * B, B)
     start(b_7t, b_7b)
     stage(X2 * B, B)
     start(b_6t, b_6b)
-    tiles(OWN, 6, T2L, 2)
-    put(G3L, text_sum(T3L))
-    start(b_c3l)
+    tile(YXM * B, 2 * B, T2L, 2)
     stage(YXM * B + HALF, HALF)
     start(b_4[1:])
     stage(YXP * B, HALF)
     start(b_5[:1])
-    put(G3F, text_sum(T3F))
-    start(b_c3f)
+    tile(OWN * B, 4 * B, T2L, 2)
+    for k in range(2):
+        put(G3L, text_sum(T3L, k, HALF), k)
+        start(b_c3l[k : k + 1])
     sl[pl.ds(0, 8), :] = loss[...]
     start(l_c)
-
-    for k in range(2):
-        if k == 0:
-            landed(b_c3l)
-        put(G2L, text_sum(T2L, k, HALF) + got(G3L, k, HALF), k)
-        start(b_p2l[k : k + 1])
 
     landed(b_7t)
     stage_sum(YXM * B, 0)
@@ -298,16 +331,10 @@
     stage_sum(YXP * B + HALF, 1)
     start(b_5[1:])
 
-    put(G1A, text_sum(T1A))
-    put(G1B, text_sum(T1B))
-    start(b_c1)
-    landed(b_c3f)
-    put(G2F, text_sum(T2F) + got(G3F))
-    landed(l_c)
-    loss_2f = loss[pl.ds(T2F, 1), :] + rl[pl.ds(T3F, 1), :]
-    loss_2l = loss[pl.ds(T2L, 1), :] + rl[pl.ds(T3L, 1), :]
-    sl[pl.ds(8, 8), :] = jnp.concatenate([loss_2f, loss_2l] * 4, axis=0)
-    start(l_p)
+    for k in range(2):
+        landed(b_c3l[k : k + 1])
+        put(G2L, text_sum(T2L, k, HALF) + got(G3L, k, HALF), k)
+        start(b_p2l[k : k + 1])
 
     stage(XM * B + HALF, HALF)
     start(b_1[1:])
@@ -320,11 +347,18 @@
     stage_sum(XP * B + HALF, 3)
     start(b_2[1:])
 
+    landed(b_c3f)
+    put(G2F, text_sum(T2F) + got(G3F))
+    landed(l_c)
+    loss_2f = loss[pl.ds(T2F, 1), :] + rl[pl.ds(T3F, 1), :]
+    loss_2l = loss[pl.ds(T2L, 1), :] + rl[pl.ds(T3L, 1), :]
+    sl[pl.ds(8, 8), :] = jnp.concatenate([loss_2f, loss_2l] * 4, axis=0)
+    start(l_p)
+    left(b_p2l)
+    start(b_p2f)
+
     odd = core.astype(jnp.float32)
     high = y_lo.astype(jnp.float32)
-    for c in b_p2l:
-        c.wait_send()
-    start(b_p2f)
     landed(b_c1)
     for k in range(2):
         landed(b_p2l[k : k + 1])
@@ -386,9 +420,19 @@
         + rl[pl.ds(8, 1), :] * (1.0 - high)
         + rl[pl.ds(24, 1), :]
     ) * (1.0 / STEPS)
-    for c in sent:
-        if all(c is not done for done in b_p2l):
-            c.wait_send()
+
+    left(f_xp, f_xm, f_y, f_x2t, f_x2b, f_yxp, f_yxm, f_yx2t, f_yx2b)
+    left(f_z1, f_c1a, f_c1b, f_p2f, f_c3f, f_c3l)
+    left(b_7t, b_7b, b_6t, b_6b, b_4, b_5, b_1, b_2, b_3)
+    left(b_c3l, b_c3f, b_c1, b_p2f, b_zr, b_zs, l_c, l_p, l_zr, l_zs)
+
+    @pl.when(core == 1)
+    def _():
+        left(f_z2)
+
+    @pl.when(y_lo == 0)
+    def _():
+        left(f_p2l, f_zf)
 
 
 SEMS = 80

time: 72.7 us -> 70.1 us (0.964)
  the two profiles are of different devices: /device:TPU:1 before, /device:TPU:6 now
where the time goes in v4:
time: 70.1 us; the launch traced here: 70 us
  Pallas kernels  65.9 us (94%)
  local copies, waits for them, and re-layouts  2.14 us (3%)
  between operations  1.93 us (3%)
    pallas_call x1, Pallas kernels, on_device(): pl.pallas_call(kernel, out_shape=(jax.ShapeDtypeStruct((B, width), jnp.fl...  65.9 us
    unnamed x3, local copies, waits for them, and re-layouts  2.14 us

profile of v4, /device:TPU:6, one launch (start us, length us, event | category | flops | bytes accessed | tf_op | source)
XLA Modules:
  0.0 70.0 jit_solution(613884564564700061)
XLA Ops:
  1.9 65.9 %window.1 = (f32[128,1152]{1,0:T(8,128)S(1)}, f32[128,1152]{1,0:T(8,128)S(1)}, f32[1,128]{1,0:T(1,128)S(1)}) custom-call(bf16[128,1152]{1,0:T(8,128)(2,1)} %images_in.1, bf16[128,1152]{1,0:T(8,128)(2,1)} %texts_in.1, f32[1]{0:T(128)S(6)} %copy.10.log_scale, f32[1]{0:T(128)S(6)} %copy.11.bias), custom_call_target="tpu_custom_call" | custom-call | tf_op jit(solution)/shard_map/window/pallas_call | solution.py:448
  67.8 0.8 %copy.12 = f32[128,1152]{1,0:T(8,128)} copy(f32[128,1152]{1,0:T(8,128)S(1)} %get-tuple-element.12) | data formatting | bytes 1179648
  68.6 0.8 %copy.13 = f32[128,1152]{1,0:T(8,128)} copy(f32[128,1152]{1,0:T(8,128)S(1)} %get-tuple-element.13) | data formatting | bytes 1179648
  69.5 0.5 copy.14

commit v5 on v4

--- a/solution.py
+++ b/solution.py
@@ -8,6 +8,7 @@
 STEPS = 8
 B = 128
 HALF = B // 2
+QUARTER = B // 4
 MESH = pl.DeviceIdType.MESH
 
 OWN, XM, XP, Y, YXM, YXP, X2, YX2 = range(8)
@@ -81,8 +82,9 @@
     f_x2b = copies(img, XP * B + HALF, img, X2 * B + HALF, HALF, at_xm)
     f_yxp = copies(img, Y * B, img, YXM * B, B, at_xp, 2)
     f_yxm = copies(img, Y * B, img, YXP * B, B, at_xm, 2)
-    f_yx2t = copies(img, YXM * B, img, YX2 * B, HALF, at_xp)
-    f_yx2b = copies(img, YXP * B + HALF, img, YX2 * B + HALF, HALF, at_xm)
+    f_yx2t = copies(img, YXM * B, img, YX2 * B, QUARTER, at_xp)
+    f_yx2b = copies(img, YXP * B + 3 * QUARTER, img, YX2 * B + 3 * QUARTER, QUARTER, at_xm)
+    f_yx2y = copies(img, X2 * B + QUARTER, img, YX2 * B + QUARTER, HALF, at_y)
     f_z1 = copies(txt, T0B * B, txt, T0A * B, B, at_zp, 2)
     f_c1a = copies(txt, T0A * B, txt, T1A * B, B, at_core)
     f_z2 = copies(txt, T0A * B, txt, RELAY * B, B, at_zp, 2)
@@ -92,26 +94,30 @@
     f_zf = copies(txt, T2F * B, txt, T2L * B, B, at_zp, 2)
     f_c3f = copies(txt, T2F * B, txt, T3F * B, B, at_core)
     f_c3l = copies(txt, T2L * B, txt, T3L * B, B, at_core, 2)
-    b_7t = copies(sp, YX2 * B, rxh, 0, HALF, at_xm)
-    b_7b = copies(sp, YX2 * B + HALF, rxh, HALF, HALF, at_xp)
-    b_6t = copies(sp, X2 * B, rxh, 2 * HALF, HALF, at_xm)
-    b_6b = copies(sp, X2 * B + HALF, rxh, 3 * HALF, HALF, at_xp)
-    b_4 = copies(sp, YXM * B, rx, 0 * B, B, at_xm, 2)
-    b_5 = copies(sp, YXP * B, rx, 1 * B, B, at_xp, 2)
+    b_7t = copies(sp, YX2 * B, rxh, 0, QUARTER, at_xm)
+    b_7y = copies(sp, YX2 * B + QUARTER, rxh, QUARTER, HALF, at_y)
+    b_7b = copies(sp, YX2 * B + 3 * QUARTER, rxh, 3 * QUARTER, QUARTER, at_xp)
+    b_6t = copies(sp, X2 * B, rxh, B, HALF, at_xm)
+    b_6b = copies(sp, X2 * B + HALF, rxh, B + HALF, HALF, at_xp)
+    b_4s = copies(sp, YXM * B, rx, 0, QUARTER, at_xm)
+    b_4 = copies(sp, YXM * B + QUARTER, rx, QUARTER, 3 * QUARTER, at_xm)
+    b_5 = copies(sp, YXP * B, rx, B, 3 * QUARTER, at_xp)
+    b_5s = copies(sp, YXP * B + 3 * QUARTER, rx, B + 3 * QUARTER, QUARTER, at_xp)
     b_1 = copies(sp, XM * B, rx, 2 * B, B, at_xm, 2)
     b_2 = copies(sp, XP * B, rx, 3 * B, B, at_xp, 2)
     b_3 = copies(sp, Y * B, rx, 4 * B, B, at_y, 2)
     b_c3l = copies(sg, G3L * B, rg, G3L * B, B, at_core, 2)
     b_c3f = copies(sg, G3F * B, rg, G3F * B, B, at_core)
     b_c1 = copies(sg, G1A * B, rg, G1A * B, 2 * B, at_core)
-    b_p2l = copies(sg, G2L * B, rg, G2L * B, B, at_pair, 2)
+    b_zf = copies(sg, G2L * B, rg, G2L * B, B, at_zm, 2)
     b_p2f = copies(sg, G2F * B, rg, G2F * B, B, at_pair, 2)
-    b_zr = copies(sg, GR * B, rg, GR * B, B, at_zm, 2)
+    b_zr = copies(rg, G1B * B, rg, GR * B, B, at_zm, 2)
     b_zs = copies(sg, GS * B, rg, GS * B, B, at_zm, 2)
     l_c = copies(sl, 0, rl, 0, 8, at_core)
-    l_p = copies(sl, 8, rl, 8, 8, at_pair)
-    l_zr = copies(sl, 16, rl, 16, 8, at_zm)
-    l_zs = copies(sl, 24, rl, 24, 8, at_zm)
+    l_zf = copies(sl, 8, rl, 8, 8, at_zm)
+    l_p = copies(sl, 16, rl, 16, 8, at_pair)
+    l_zr = copies(rl, 0, rl, 24, 8, at_zm)
+    l_zs = copies(sl, 24, rl, 32, 8, at_zm)
 
     def start(*lists):
         for group in lists:
@@ -207,7 +213,7 @@
         if k == 0:
             start(f_yxp[:1])
         else:
-            start(f_yxm[1:], f_yxm[:1], f_yxp[1:])
+            start(f_yxm[1:])
 
             @pl.when(y_lo == 0)
             def _():
@@ -215,7 +221,7 @@
 
     def round_x():
         landed(f_xp, f_xm)
-        start(f_x2t, f_x2b)
+        start(f_x2t, f_x2b, f_yxm[:1], f_yxp[1:])
 
     def round_yx():
         landed(f_yxp[:1])
@@ -229,8 +235,12 @@
         from_y(1)
         round_x()
         round_yx()
-        from_z(0)
-        from_z(1)
+        for k in range(2):
+            from_z(k)
+
+            @pl.when(y_lo == 0)
+            def _():
+                start(f_p2l[k : k + 1])
 
     @pl.when(z > 0)
     def _():
@@ -243,17 +253,22 @@
     start(f_c1a)
     tile(OWN * B, 4 * B, T0B, 2, diagonal=True)
 
+    up_z = jnp.logical_or(y_lo == 0, z < n_blk // 4 - 1)
+    from_below = jnp.logical_or(y_lo == 0, z > 0)
+
+    def forward(k):
+        landed(f_p2f[k : k + 1])
+
+        @pl.when(up_z)
+        def _():
+            start(f_zf[k : k + 1])
+
+    forward(0)
+
     @pl.when(z > 0)
     def _():
         round_yx()
 
-    @pl.when(y_lo == 0)
-    def _():
-        start(f_p2l)
-        landed(f_p2f[:1])
-        start(f_zf[:1])
-        landed(f_p2f[1:])
-        start(f_zf[1:])
 
     @pl.when(core == 1)
     def _():
@@ -262,24 +277,19 @@
 
     landed(f_c1a, f_c1b)
     tile(OWN * B, 4 * B, T1A, 2)
-
-    @pl.when(y_lo == 1)
-    def _():
-        landed(f_p2f)
-
+    landed(f_x2t, f_x2b)
+    start(f_yx2y)
+    forward(1)
     start(f_c3f)
     landed(f_yxp[1:], f_yxm[:1], f_c3f)
     tile(OWN * B, 4 * B, T2F, 2)
     tile(YXM * B, 2 * B, T0B, 6)
-    landed(f_x2t, f_x2b, f_yx2t, f_yx2b)
-    tile(X2 * B, 2 * B, T0B, 6)
-
     def stage(row, rows):
         sp[pl.ds(row, rows), :] = pg[pl.ds(row, rows), :].astype(jnp.bfloat16)
 
-    def stage_sum(row, half):
-        total = pg[pl.ds(row, HALF), :] + rxh[pl.ds(half * HALF, HALF), :].astype(jnp.float32)
-        sp[pl.ds(row, HALF), :] = total.astype(jnp.bfloat16)
+    def stage_sum(row, at, rows):
+        total = pg[pl.ds(row, rows), :] + rxh[pl.ds(at, rows), :].astype(jnp.float32)
+        sp[pl.ds(row, rows), :] = total.astype(jnp.bfloat16)
 
     def text_sum(slot, k=0, rows=B):
         return tgr[pl.ds(slot * B + k * HALF, rows), :]
@@ -290,87 +300,145 @@
     def got(slot, k=0, rows=B):
         return rg[pl.ds(slot * B + k * HALF, rows), :].astype(jnp.float32)
 
-    for k in range(2):
-
-        @pl.when(y_lo == 0)
-        def _():
-            landed(f_zf[k : k + 1])
-
-        @pl.when(y_lo == 1)
-        def _():
-            landed(f_p2l[k : k + 1])
-
-        start(f_c3l[k : k + 1])
-    put(G3F, text_sum(T3F))
-    start(b_c3f)
-    put(G1A, text_sum(T1A))
-    put(G1B, text_sum(T1B))
-    start(b_c1)
-    landed(f_c3l)
-    tile(X2 * B, 2 * B, T2L, 2)
-    stage(YX2 * B, B)
-    start(b_7t, b_7b)
-    stage(X2 * B, B)
-    start(b_6t, b_6b)
-    tile(YXM * B, 2 * B, T2L, 2)
-    stage(YXM * B + HALF, HALF)
-    start(b_4[1:])
-    stage(YXP * B, HALF)
-    start(b_5[:1])
-    tile(OWN * B, 4 * B, T2L, 2)
-    for k in range(2):
-        put(G3L, text_sum(T3L, k, HALF), k)
-        start(b_c3l[k : k + 1])
-    sl[pl.ds(0, 8), :] = loss[...]
-    start(l_c)
-
-    landed(b_7t)
-    stage_sum(YXM * B, 0)
-    start(b_4[:1])
-    landed(b_7b)
-    stage_sum(YXP * B + HALF, 1)
-    start(b_5[1:])
-
+    def last_texts():
+        for k in range(2):
+
+            @pl.when(from_below)
+            def _():
+                landed(f_zf[k : k + 1])
+
+            @pl.when(jnp.logical_not(from_below))
+            def _():
+                landed(f_p2l[k : k + 1])
+
+            start(f_c3l[k : k + 1])
+
+    def ready_texts():
+        put(G1A, text_sum(T1A))
+        put(G1B, text_sum(T1B))
+        start(b_c1)
+        put(G3F, text_sum(T3F))
+        start(b_c3f)
+
+    def far_images():
+        stage(YX2 * B, B)
+        start(b_7t, b_7b, b_7y)
+
+    def far_texts():
+        for k in range(2):
+            put(G3L, text_sum(T3L, k, HALF), k)
+            start(b_c3l[k : k + 1])
+
+    @pl.when(z == 0)
+    def _():
+        landed(f_yx2t, f_yx2b, f_yx2y)
+        tile(X2 * B, 2 * B, T0B, 6)
+        last_texts()
+        ready_texts()
+        landed(f_c3l)
+        tile(X2 * B, 2 * B, T2L, 2)
+        far_images()
+        tile(YXM * B, 2 * B, T2L, 2)
+        tile(OWN * B, 4 * B, T2L, 2)
+        far_texts()
+
+    @pl.when(z > 0)
+    def _():
+        last_texts()
+        landed(f_c3l)
+        tile(OWN * B, 4 * B, T2L, 2)
+        landed(f_yx2t, f_yx2b, f_yx2y)
+        tile(X2 * B, 2 * B, T0B, 8)
+        far_images()
+        tile(YXM * B, 2 * B, T2L, 2)
+        far_texts()
+        ready_texts()
+
+    stage(YXM * B + QUARTER, 3 * QUARTER)
+    start(b_4)
+    stage(YXP * B, 3 * QUARTER)
+    start(b_5)
     for k in range(2):
         landed(b_c3l[k : k + 1])
         put(G2L, text_sum(T2L, k, HALF) + got(G3L, k, HALF), k)
-        start(b_p2l[k : k + 1])
-
+        start(b_zf[k : k + 1])
+    landed(b_c1)
+
+    @pl.when(core == 1)
+    def _():
+        start(b_zr)
+
+    landed(b_7t)
+    stage_sum(YXM * B, 0, QUARTER)
+    start(b_4s)
+    landed(b_7b)
+    stage_sum(YXP * B + 3 * QUARTER, 3 * QUARTER, QUARTER)
+    start(b_5s)
+    landed(b_7y)
+    stage(X2 * B, QUARTER)
+    stage_sum(X2 * B + QUARTER, QUARTER, HALF)
+    stage(X2 * B + 3 * QUARTER, QUARTER)
+    start(b_6t, b_6b)
+
+    sl[pl.ds(0, 8), :] = loss[...]
+    start(l_c)
     stage(XM * B + HALF, HALF)
     start(b_1[1:])
     stage(XP * B, HALF)
     start(b_2[:1])
+    landed(b_c3f, l_c)
+    loss_2f = loss[pl.ds(T2F, 1), :] + rl[pl.ds(T3F, 1), :]
+    loss_2l = loss[pl.ds(T2L, 1), :] + rl[pl.ds(T3L, 1), :]
+    sl[pl.ds(8, 8), :] = jnp.broadcast_to(loss_2l, (8, B))
+    start(l_zf)
+
+    @pl.when(core == 1)
+    def _():
+        start(l_zr)
+
+    for k in range(2):
+        landed(b_zf[k : k + 1])
+        total = text_sum(T2F, k, HALF) + got(G3F, k, HALF) + got(G2L, k, HALF)
+        put(G2F, total, k)
+        start(b_p2f[k : k + 1])
+    landed(l_zf)
+    sl[pl.ds(16, 8), :] = jnp.broadcast_to(loss_2f + rl[pl.ds(8, 1), :], (8, B))
+    start(l_p)
+
+    tgr[pl.ds(T0A * B, B), :] += got(G1A)
+    loss[pl.ds(T0A, 1), :] += rl[pl.ds(T1A, 1), :]
+
+    @pl.when(core == 1)
+    def _():
+        landed(b_zr, l_zr)
+        tgr[pl.ds(T0A * B, B), :] += got(GR)
+        loss[pl.ds(T0A, 1), :] += rl[pl.ds(24 + T1B, 1), :]
+
+    def down_z(k, add):
+        value = text_sum(T0A, k, HALF)
+        if add:
+            value += got(G2F, k, HALF)
+        put(GS, value, k)
+        start(b_zs[k : k + 1])
+
+    @pl.when(y_lo == 0)
+    def _():
+        down_z(0, False)
+        down_z(1, False)
+
     landed(b_6t)
-    stage_sum(XM * B, 2)
+    stage_sum(XM * B, B, HALF)
     start(b_1[:1])
     landed(b_6b)
-    stage_sum(XP * B + HALF, 3)
+    stage_sum(XP * B + HALF, B + HALF, HALF)
     start(b_2[1:])
 
-    landed(b_c3f)
-    put(G2F, text_sum(T2F) + got(G3F))
-    landed(l_c)
-    loss_2f = loss[pl.ds(T2F, 1), :] + rl[pl.ds(T3F, 1), :]
-    loss_2l = loss[pl.ds(T2L, 1), :] + rl[pl.ds(T3L, 1), :]
-    sl[pl.ds(8, 8), :] = jnp.concatenate([loss_2f, loss_2l] * 4, axis=0)
-    start(l_p)
-    left(b_p2l)
-    start(b_p2f)
-
-    odd = core.astype(jnp.float32)
-    high = y_lo.astype(jnp.float32)
-    landed(b_c1)
-    for k in range(2):
-        landed(b_p2l[k : k + 1])
-        put(GR, got(G1B, k, HALF) * odd + got(G2L, k, HALF) * high, k)
-        start(b_zr[k : k + 1])
-    landed(l_p)
-    sl[pl.ds(16, 8), :] = jnp.broadcast_to(
-        rl[pl.ds(T1B, 1), :] * odd + rl[pl.ds(9, 1), :] * high, (8, B)
-    )
-    start(l_zr)
-
-    landed(b_4, b_5)
+    @pl.when(y_lo == 1)
+    def _():
+        landed(b_p2f[:1])
+        down_z(0, True)
+
+    landed(b_4, b_5, b_4s, b_5s)
     for k in range(2):
         total = (
             pg[pl.ds(Y * B + k * HALF, HALF), :]
@@ -380,21 +448,27 @@
         sp[pl.ds(Y * B + k * HALF, HALF), :] = total.astype(jnp.bfloat16)
         start(b_3[k : k + 1])
 
-    for k in range(2):
-        landed(b_p2f[k : k + 1], b_zr[k : k + 1])
-        from_pair = got(G2F, k, HALF) * high + got(G2L, k, HALF) * (1.0 - high)
-        put(GS, text_sum(T0A, k, HALF) + got(G1A, k, HALF) + from_pair + got(GR, k, HALF), k)
-        start(b_zs[k : k + 1])
-    landed(l_zr)
-    sl[pl.ds(24, 8), :] = jnp.broadcast_to(
-        loss[pl.ds(T0A, 1), :]
-        + rl[pl.ds(T1A, 1), :]
-        + rl[pl.ds(8, 1), :] * high
-        + rl[pl.ds(9, 1), :] * (1.0 - high)
-        + rl[pl.ds(16, 1), :],
-        (8, B),
-    )
+    landed(l_p)
+
+    @pl.when(y_lo == 1)
+    def _():
+        landed(b_p2f[1:])
+        down_z(1, True)
+        loss[pl.ds(T0A, 1), :] += rl[pl.ds(16, 1), :]
+
+    sl[pl.ds(24, 8), :] = jnp.broadcast_to(loss[pl.ds(T0A, 1), :], (8, B))
     start(l_zs)
+
+    @pl.when(y_lo == 0)
+    def _():
+        landed(b_p2f)
+        tgr[pl.ds(T0B * B, B), :] += got(G2F)
+        loss[pl.ds(T0B, 1), :] += rl[pl.ds(16, 1), :]
+
+    @pl.when(core == 0)
+    def _():
+        tgr[pl.ds(T0B * B, B), :] += got(G1B)
+        loss[pl.ds(T0B, 1), :] += rl[pl.ds(T1B, 1), :]
 
     wide_temper = jnp.concatenate([temper] * (images.shape[1] // B), axis=1)
 
@@ -409,30 +483,26 @@
     image_grad[...] = chain_back(unit, inverse, wide_temper * image_sum)
 
     landed(b_zs, l_zs)
-    own_sum = (
-        text_sum(T0B) + got(G1B) * (1.0 - odd) + got(G2F) * (1.0 - high) + got(GS)
-    )
     unit, inverse = normalized(texts)
-    text_grad[...] = chain_back(unit, inverse, wide_temper * own_sum)
-    text_loss[...] = (
-        loss[pl.ds(T0B, 1), :]
-        + rl[pl.ds(T1B, 1), :] * (1.0 - odd)
-        + rl[pl.ds(8, 1), :] * (1.0 - high)
-        + rl[pl.ds(24, 1), :]
-    ) * (1.0 / STEPS)
-
-    left(f_xp, f_xm, f_y, f_x2t, f_x2b, f_yxp, f_yxm, f_yx2t, f_yx2b)
+    text_grad[...] = chain_back(unit, inverse, wide_temper * (text_sum(T0B) + got(GS)))
+    text_loss[...] = (loss[pl.ds(T0B, 1), :] + rl[pl.ds(32, 1), :]) * (1.0 / STEPS)
+
+    left(f_xp, f_xm, f_y, f_x2t, f_x2b, f_yxp, f_yxm, f_yx2t, f_yx2b, f_yx2y)
     left(f_z1, f_c1a, f_c1b, f_p2f, f_c3f, f_c3l)
-    left(b_7t, b_7b, b_6t, b_6b, b_4, b_5, b_1, b_2, b_3)
-    left(b_c3l, b_c3f, b_c1, b_p2f, b_zr, b_zs, l_c, l_p, l_zr, l_zs)
+    left(b_7t, b_7b, b_7y, b_6t, b_6b, b_4, b_5, b_4s, b_5s, b_1, b_2, b_3)
+    left(b_c3l, b_c3f, b_c1, b_p2f, b_zf, b_zs, l_c, l_p, l_zf, l_zs)
 
     @pl.when(core == 1)
     def _():
-        left(f_z2)
-
-    @pl.when(y_lo == 0)
-    def _():
-        left(f_p2l, f_zf)
+        left(f_z2, b_zr, l_zr)
+
+    @pl.when(up_z)
+    def _():
+        left(f_zf)
+
+    @pl.when(jnp.logical_and(z == 0, y_lo == 0))
+    def _():
+        left(f_p2l)
 
 
 SEMS = 80
@@ -445,6 +515,7 @@
     rows = lambda n, dtype: pltpu.VMEM((n, width), dtype)
     vmem = pl.BlockSpec(memory_space=pltpu.VMEM)
     smem = pl.BlockSpec(memory_space=pltpu.SMEM)
+    hbm = pl.BlockSpec(memory_space=pltpu.HBM)
     image_grad, text_grad, text_loss = pl.pallas_call(
         kernel,
         out_shape=(
@@ -452,7 +523,7 @@
             jax.ShapeDtypeStruct((B, width), jnp.float32),
             jax.ShapeDtypeStruct((1, B), jnp.float32),
         ),
-        in_specs=[pl.BlockSpec(memory_space=pltpu.HBM)] * 2 + [smem, smem],
+        in_specs=[hbm, hbm, smem, smem],
         out_specs=(vmem, vmem, vmem),
         scratch_shapes=[
             rows(B, jnp.bfloat16),
@@ -468,7 +539,7 @@
             rows(8 * B, jnp.bfloat16),
             rows(8 * B, jnp.bfloat16),
             pltpu.VMEM((32, B), jnp.float32),
-            pltpu.VMEM((32, B), jnp.float32),
+            pltpu.VMEM((40, B), jnp.float32),
             pltpu.SemaphoreType.DMA((2,)),
             pltpu.SemaphoreType.DMA((SEMS,)),
             pltpu.SemaphoreType.DMA((SEMS,)),

time: 70.1 us -> 68.7 us (0.980)
  the two profiles are of different devices: /device:TPU:6 before, /device:TPU:1 now
where the time goes in v5:
time: 68.7 us; the launch traced here: 68.5 us
  Pallas kernels  64.5 us (94%)
  local copies, waits for them, and re-layouts  2.14 us (3%)
  between operations  1.93 us (3%)
    pallas_call x1, Pallas kernels, on_device(): pl.pallas_call(kernel, out_shape=(jax.ShapeDtypeStruct((B, width), jnp.fl...  64.5 us
    unnamed x3, local copies, waits for them, and re-layouts  2.14 us

profile of v5, /device:TPU:1, one launch (start us, length us, event | category | flops | bytes accessed | tf_op | source)
XLA Modules:
  0.0 68.5 jit_solution(11067686321904073144)
XLA Ops:
  1.9 64.5 %window.1 = (f32[128,1152]{1,0:T(8,128)S(1)}, f32[128,1152]{1,0:T(8,128)S(1)}, f32[1,128]{1,0:T(1,128)S(1)}) custom-call(bf16[128,1152]{1,0:T(8,128)(2,1)} %images_in.1, bf16[128,1152]{1,0:T(8,128)(2,1)} %texts_in.1, f32[1]{0:T(128)S(6)} %copy.10.log_scale, f32[1]{0:T(128)S(6)} %copy.11.bias), custom_call_target="tpu_custom_call" | custom-call | tf_op jit(solution)/shard_map/window/pallas_call | solution.py:519
  66.4 0.8 %copy.12 = f32[128,1152]{1,0:T(8,128)} copy(f32[128,1152]{1,0:T(8,128)S(1)} %get-tuple-element.12) | data formatting | bytes 1179648
  67.2 0.8 %copy.13 = f32[128,1152]{1,0:T(8,128)} copy(f32[128,1152]{1,0:T(8,128)S(1)} %get-tuple-element.13) | data formatting | bytes 1179648
  68.0 0.5 copy.14

commit v6 on v5

--- a/solution.py
+++ b/solution.py
@@ -16,8 +16,8 @@
 G1A, G1B, G2F, G2L, G3F, G3L, GR, GS = range(8)
 
 
-def normalized(ref):
-    wide = ref[...].astype(jnp.float32)
+def normalized(values):
+    wide = values.astype(jnp.float32)
     inverse = lax.rsqrt(jnp.sum(wide * wide, axis=-1, keepdims=True) + 1e-06)
     return wide * inverse, inverse
 
@@ -28,7 +28,7 @@
 
 def kernel(
     images_in, texts_in, log_scale, bias, image_grad, text_grad, text_loss,
-    images, texts, img, txt, pg, tgr, loss, sp, rxh, rx, sg, rg, sl, rl, isem, ssem, rsem,
+    images, texts, img, txt, kept, pg, tgr, loss, sp, rxh, rx, sg, rg, sl, rl, isem, ssem, rsem,
 ):
     blk, member = lax.axis_index("blk"), lax.axis_index("member")
     n_blk, n_member = lax.axis_size("blk"), lax.axis_size("member")
@@ -77,11 +77,15 @@
 
     f_xp = copies(img, OWN * B, img, XM * B, B, at_xp, 2)
     f_xm = copies(img, OWN * B, img, XP * B, B, at_xm, 2)
-    f_y = copies(img, OWN * B, img, Y * B, B, at_y, 2)
+    outer = (0, 3 * QUARTER)
+    f_yo = [c for r in outer for c in copies(img, OWN * B + r, img, Y * B + r, QUARTER, at_y)]
+    f_ym = copies(img, OWN * B + QUARTER, img, Y * B + QUARTER, HALF, at_y)
     f_x2t = copies(img, XM * B, img, X2 * B, HALF, at_xp)
     f_x2b = copies(img, XP * B + HALF, img, X2 * B + HALF, HALF, at_xm)
-    f_yxp = copies(img, Y * B, img, YXM * B, B, at_xp, 2)
-    f_yxm = copies(img, Y * B, img, YXP * B, B, at_xm, 2)
+    f_yxpo = [c for r in outer for c in copies(img, Y * B + r, img, YXM * B + r, QUARTER, at_xp)]
+    f_yxmo = [c for r in outer for c in copies(img, Y * B + r, img, YXP * B + r, QUARTER, at_xm)]
+    f_yxp = copies(img, Y * B + QUARTER, img, YXM * B + QUARTER, HALF, at_xp)
+    f_yxm = copies(img, Y * B + QUARTER, img, YXP * B + QUARTER, HALF, at_xm)
     f_yx2t = copies(img, YXM * B, img, YX2 * B, QUARTER, at_xp)
     f_yx2b = copies(img, YXP * B + 3 * QUARTER, img, YX2 * B + 3 * QUARTER, QUARTER, at_xm)
     f_yx2y = copies(img, X2 * B + QUARTER, img, YX2 * B + QUARTER, HALF, at_y)
@@ -142,16 +146,16 @@
     offset = bias[0]
 
     text_load.wait()
-    unit, _ = normalized(texts)
+    unit, _ = normalized(texts[...])
     txt[pl.ds(T0B * B, B), :] = unit.astype(jnp.bfloat16)
 
     pl.semaphore_wait(barrier, len(partners))
 
     start(f_z1)
     image_load.wait()
-    unit, _ = normalized(images)
+    unit, _ = normalized(images[...])
     img[pl.ds(OWN * B, B), :] = unit.astype(jnp.bfloat16)
-    start(f_y, f_xp, f_xm)
+    start(f_yo, f_ym, f_xp, f_xm)
 
     @pl.when(core == 0)
     def _():
@@ -161,7 +165,7 @@
     tgr[...] = jnp.zeros_like(tgr)
     loss[...] = jnp.zeros_like(loss)
 
-    def tile(row, rows, first, blocks, diagonal=False):
+    def tile(row, rows, first, blocks, diagonal=False, keep=False):
         cols = blocks * B
         i = img[pl.ds(row, rows), :]
         t = txt[pl.ds(first * B, cols), :]
@@ -193,6 +197,12 @@
             loss[pl.ds(first + k, 1), :] += column[:, k * B : (k + 1) * B]
         low = slope.astype(jnp.bfloat16)
         pg[pl.ds(row, rows), :] += jnp.dot(low, t, preferred_element_type=jnp.float32)
+        if keep:
+            kept[:, pl.ds(0, cols)] = low
+        else:
+            text_part(low, i, first, cols)
+
+    def text_part(low, i, first, cols):
         tgr[pl.ds(first * B, cols), :] += lax.dot_general(
             low, i, (((0,), (0,)), ((), ())), preferred_element_type=jnp.float32
         )
@@ -208,32 +218,33 @@
         def _():
             start_choice(f_p2f[k : k + 1], 1)
 
-    def from_y(k):
-        landed(f_y[k : k + 1])
-        if k == 0:
-            start(f_yxp[:1])
-        else:
-            start(f_yxm[1:])
-
-            @pl.when(y_lo == 0)
-            def _():
-                start_choice(f_p2f, 0)
+    def from_y_outer():
+        landed(f_yo)
+        start(f_yxpo[:1], f_yxmo[1:], f_yxpo[1:], f_yxmo[:1])
+
+    def from_y_middle():
+        landed(f_ym)
+        start(f_yxp, f_yxm)
+
+        @pl.when(y_lo == 0)
+        def _():
+            start_choice(f_p2f, 0)
 
     def round_x():
         landed(f_xp, f_xm)
-        start(f_x2t, f_x2b, f_yxm[:1], f_yxp[1:])
+        start(f_x2t, f_x2b)
 
     def round_yx():
-        landed(f_yxp[:1])
+        landed(f_yxpo[:1])
         start(f_yx2t)
-        landed(f_yxm[1:])
+        landed(f_yxmo[1:])
         start(f_yx2b)
 
     @pl.when(z == 0)
     def _():
-        from_y(0)
-        from_y(1)
+        from_y_outer()
         round_x()
+        from_y_middle()
         round_yx()
         for k in range(2):
             from_z(k)
@@ -245,13 +256,17 @@
     @pl.when(z > 0)
     def _():
         from_z(0)
-        from_y(0)
+        from_y_outer()
         from_z(1)
-        from_y(1)
         round_x()
+        from_y_middle()
 
     start(f_c1a)
     tile(OWN * B, 4 * B, T0B, 2, diagonal=True)
+
+    @pl.when(z > 0)
+    def _():
+        round_yx()
 
     up_z = jnp.logical_or(y_lo == 0, z < n_blk // 4 - 1)
     from_below = jnp.logical_or(y_lo == 0, z > 0)
@@ -264,10 +279,6 @@
             start(f_zf[k : k + 1])
 
     forward(0)
-
-    @pl.when(z > 0)
-    def _():
-        round_yx()
 
 
     @pl.when(core == 1)
@@ -281,7 +292,7 @@
     start(f_yx2y)
     forward(1)
     start(f_c3f)
-    landed(f_yxp[1:], f_yxm[:1], f_c3f)
+    landed(f_yxpo[1:], f_yxmo[:1], f_yxp, f_yxm, f_c3f)
     tile(OWN * B, 4 * B, T2F, 2)
     tile(YXM * B, 2 * B, T0B, 6)
     def stage(row, rows):
@@ -329,30 +340,16 @@
             put(G3L, text_sum(T3L, k, HALF), k)
             start(b_c3l[k : k + 1])
 
-    @pl.when(z == 0)
-    def _():
-        landed(f_yx2t, f_yx2b, f_yx2y)
-        tile(X2 * B, 2 * B, T0B, 6)
-        last_texts()
-        ready_texts()
-        landed(f_c3l)
-        tile(X2 * B, 2 * B, T2L, 2)
-        far_images()
-        tile(YXM * B, 2 * B, T2L, 2)
-        tile(OWN * B, 4 * B, T2L, 2)
-        far_texts()
-
-    @pl.when(z > 0)
-    def _():
-        last_texts()
-        landed(f_c3l)
-        tile(OWN * B, 4 * B, T2L, 2)
-        landed(f_yx2t, f_yx2b, f_yx2y)
-        tile(X2 * B, 2 * B, T0B, 8)
-        far_images()
-        tile(YXM * B, 2 * B, T2L, 2)
-        far_texts()
-        ready_texts()
+    last_texts()
+    landed(f_c3l)
+    tile(OWN * B, 4 * B, T2L, 2)
+    landed(f_yx2t, f_yx2b, f_yx2y)
+    tile(X2 * B, 2 * B, T0B, 8, keep=True)
+    far_images()
+    text_part(kept[...], img[pl.ds(X2 * B, 2 * B), :], T0B, 8 * B)
+    tile(YXM * B, 2 * B, T2L, 2)
+    far_texts()
+    ready_texts()
 
     stage(YXM * B + QUARTER, 3 * QUARTER)
     start(b_4)
@@ -472,22 +469,28 @@
 
     wide_temper = jnp.concatenate([temper] * (images.shape[1] // B), axis=1)
 
-    landed(b_1, b_2, b_3)
-    image_sum = (
-        pg[pl.ds(OWN * B, B), :]
-        + rx[pl.ds(2 * B, B), :].astype(jnp.float32)
-        + rx[pl.ds(3 * B, B), :].astype(jnp.float32)
-        + rx[pl.ds(4 * B, B), :].astype(jnp.float32)
-    )
-    unit, inverse = normalized(images)
-    image_grad[...] = chain_back(unit, inverse, wide_temper * image_sum)
-
-    landed(b_zs, l_zs)
-    unit, inverse = normalized(texts)
-    text_grad[...] = chain_back(unit, inverse, wide_temper * (text_sum(T0B) + got(GS)))
+    landed(b_1, b_2)
+    pg[pl.ds(OWN * B, B), :] += rx[pl.ds(2 * B, B), :].astype(jnp.float32) + rx[
+        pl.ds(3 * B, B), :
+    ].astype(jnp.float32)
+    for k in range(2):
+        part = pl.ds(k * HALF, HALF)
+        landed(b_3[k : k + 1])
+        image_sum = pg[pl.ds(OWN * B + k * HALF, HALF), :] + rx[
+            pl.ds(4 * B + k * HALF, HALF), :
+        ].astype(jnp.float32)
+        unit, inverse = normalized(images[part, :])
+        image_grad[part, :] = chain_back(unit, inverse, wide_temper * image_sum)
+    for k in range(2):
+        part = pl.ds(k * HALF, HALF)
+        landed(b_zs[k : k + 1])
+        unit, inverse = normalized(texts[part, :])
+        total = text_sum(T0B, k, HALF) + got(GS, k, HALF)
+        text_grad[part, :] = chain_back(unit, inverse, wide_temper * total)
+    landed(l_zs)
     text_loss[...] = (loss[pl.ds(T0B, 1), :] + rl[pl.ds(32, 1), :]) * (1.0 / STEPS)
 
-    left(f_xp, f_xm, f_y, f_x2t, f_x2b, f_yxp, f_yxm, f_yx2t, f_yx2b, f_yx2y)
+    left(f_xp, f_xm, f_yo, f_ym, f_x2t, f_x2b, f_yxpo, f_yxmo, f_yxp, f_yxm, f_yx2t, f_yx2b, f_yx2y)
     left(f_z1, f_c1a, f_c1b, f_p2f, f_c3f, f_c3l)
     left(b_7t, b_7b, b_7y, b_6t, b_6b, b_4, b_5, b_4s, b_5s, b_1, b_2, b_3)
     left(b_c3l, b_c3f, b_c1, b_p2f, b_zf, b_zs, l_c, l_p, l_zf, l_zs)
@@ -530,6 +533,7 @@
             rows(B, jnp.bfloat16),
             rows(8 * B, jnp.bfloat16),
             rows(9 * B, jnp.bfloat16),
+            pltpu.VMEM((2 * B, 8 * B), jnp.bfloat16),
             rows(8 * B, jnp.float32),
             rows(8 * B, jnp.float32),
             pltpu.VMEM((8, B), jnp.float32),

time: 68.7 us -> 67.8 us (0.987)
  Pallas kernels: 64.5 us -> 63.6 us
    pallas_call x1, Pallas kernels: 64.5 us -> 63.6 us  [on_device(): pl.pallas_call(kernel, out_shape=(jax.ShapeDtypeStruct((B, width), jnp.fl...]
where the time goes in v6:
time: 67.8 us; the launch traced here: 67.7 us
  Pallas kernels  63.6 us (94%)
  local copies, waits for them, and re-layouts  2.14 us (3%)
  between operations  1.93 us (3%)
    pallas_call x1, Pallas kernels, on_device(): pl.pallas_call(kernel, out_shape=(jax.ShapeDtypeStruct((B, width), jnp.fl...  63.6 us
    unnamed x3, local copies, waits for them, and re-layouts  2.14 us

profile of v6, /device:TPU:1, one launch (start us, length us, event | category | flops | bytes accessed | tf_op | source)
XLA Modules:
  0.0 67.7 jit_solution(13637354406813827017)
XLA Ops:
  1.9 63.6 %window.1 = (f32[128,1152]{1,0:T(8,128)S(1)}, f32[128,1152]{1,0:T(8,128)S(1)}, f32[1,128]{1,0:T(1,128)S(1)}) custom-call(bf16[128,1152]{1,0:T(8,128)(2,1)} %images_in.1, bf16[128,1152]{1,0:T(8,128)(2,1)} %texts_in.1, f32[1]{0:T(128)S(6)} %copy.10.log_scale, f32[1]{0:T(128)S(6)} %copy.11.bias), custom_call_target="tpu_custom_call" | custom-call | tf_op jit(solution)/shard_map/window/pallas_call | solution.py:522
  65.5 0.8 %copy.12 = f32[128,1152]{1,0:T(8,128)} copy(f32[128,1152]{1,0:T(8,128)S(1)} %get-tuple-element.12) | data formatting | bytes 1179648
  66.3 0.8 %copy.13 = f32[128,1152]{1,0:T(8,128)} copy(f32[128,1152]{1,0:T(8,128)S(1)} %get-tuple-element.13) | data formatting | bytes 1179648
  67.1 0.5 copy.14
